TPU v7x, 32 devices: a whole 2x2x4 slice. The times are simulated.
32 devices in a mesh: row: 8 (over y, x, core), col: 4 (over z).
Axes of the slice: x: 2, y: 2, z: 4, core: 2. Of those that a mesh axis runs over, the one named last changes fastest.
Arguments:
- core_inverse: bfloat16 [20480, 20480], P('row', 'col'), as said below
- core_noncore: bfloat16 [20480, 1024], P('row', 'col'), may hold values from -3 to 3
- residual: float32 [1024], replicated, may hold values from 8 to 64
- group_live: int32 [2], replicated, may hold values from 192 to 512, as said below
Outputs:
- core_block: float32 [20480, 20480], P('row', 'col')
Inputs may be any that keep to these rules, and one draw needn't show every extreme that they name: core_inverse is exactly symmetric. `group_live`: in every draw one of the two groups holds 512 animals, the other at least 192.
All inputs are finite; a program needn't handle non-finite values.
Results may differ from a plain program's by a relative error of at most 0.0049.
Values may be sent and summed in bfloat16 or wider, within the bound.
No kernel may reach another device: no remote copies, remote signals or barrier semaphores. Data moves between devices by JAX's collectives and lax.ppermute only.
A program may use at most 192 MiB of HBM per device.

v0:
```python
import jax
import jax.numpy as jnp
from jax import lax
from jax.sharding import PartitionSpec as P

GROUP = 512


def spread(block, axis, owner):
    block = jnp.where(lax.axis_index(axis) == owner, block, jnp.zeros_like(block))
    return lax.psum(block, axis)


def shards(core_inverse, core_noncore, residual, group_live):
    row_count = core_inverse.shape[0]
    animals = lax.all_gather(core_noncore, "col", axis=1, tiled=True)
    partial_value = lax.dot_general(
        core_inverse, animals, (((0,), (0,)), ((), ())), preferred_element_type=jnp.float32
    )
    share = lax.psum_scatter(partial_value, "row", scatter_dimension=0, tiled=True).astype(
        jnp.bfloat16
    )
    column_panel = lax.all_gather(share, "row", axis=0, tiled=True)
    row_index = lax.axis_index("row")
    piece = lax.dynamic_slice_in_dim(column_panel, row_index % 2 * row_count, row_count, 0)
    row_panel = spread(piece, "col", row_index // 2)
    slots = jnp.arange(column_panel.shape[1], dtype=jnp.int32)
    limit = jnp.where(slots // GROUP == 0, group_live[0], group_live[1])
    weight = (slots % GROUP < limit).astype(jnp.float32) / residual
    scaled = (row_panel.astype(jnp.float32) * weight[None, :]).astype(jnp.bfloat16)
    update = lax.dot_general(
        scaled, column_panel, (((1,), (1,)), ((), ())), preferred_element_type=jnp.float32
    )
    return core_inverse.astype(jnp.float32) + update


def solution(mesh):
    return jax.shard_map(
        shards,
        mesh=mesh,
        in_specs=(P("row", "col"), P("row", "col"), P(), P()),
        out_specs=P("row", "col"),
        check_vma=False,
    )
```

profile of v0, /device:TPU:0, one launch (start us, length us, event | category | flops | bytes accessed | tf_op | source)
XLA Modules:
  0.0 587.1 jit_solution(3213711598042829376)
XLA Ops:
  6.5 0.0 all-gather.3.cloned.1.call-start
  6.5 0.7 all-gather.3.cloned.1.call-update
  7.3 0.0 reduce-scatter.2.cloned.1.call-start
  7.3 102.1 %all-gather.3.cloned.1.call-done = bf16[2560,1024]{1,0:T(8,128)(2,1)} async-done(((bf16[2560,256]{1,0:T(8,128)(2,1)}), bf16[2560,1024]{1,0:T(8,128)(2,1)}) %all-gather.3.cloned.1.call-update) | async-done | bytes 5242896 | tf_op jit(solution)/shard_map/all_gather | solution.py:16
  109.4 34.4 %fusion.9 = f32[5120,1024]{1,0:T(8,128)} fusion(bf16[2560,5120]{1,0:T(8,128)(2,1)} %param.4, bf16[2560,1024]{1,0:T(8,128)(2,1)} %all-gather.3.cloned.1.call-done), kind=kOutput, calls=%fused_computation.18 | convolution fusion | flops 26843545600 | bytes 52428800 | tf_op jit(solution)/shard_map/dot_general | solution.py:17
  143.8 0.0 reduce-scatter.2.cloned.1.call-update
  143.8 0.0 copy-start.1
  143.8 0.0 copy-start
  143.8 0.0 all-gather.5.cloned.1.call-start
  143.9 134.2 %reduce-scatter.2.cloned.1.call-done = f32[640,1024]{1,0:T(8,128)} async-done(((f32[5120,1024]{1,0:T(8,128)}), f32[640,1024]{1,0:T(8,128)}) %reduce-scatter.2.cloned.1.call-update) | async-done | bytes 2621456 | tf_op jit(solution)/shard_map/reduce_scatter | solution.py:20
  278.1 3.0 convert_element_type.16
  281.1 0.0 all-gather.5.cloned.1.call-update
  281.1 0.2 all-reduce.2.cloned.1.call-start
  281.4 63.2 %all-gather.5.cloned.1.call-done = bf16[5120,1024]{1,0:T(8,128)(2,1)} async-done(((bf16[640,1024]{1,0:T(8,128)(2,1)}), bf16[5120,1024]{1,0:T(8,128)(2,1)}) %all-gather.5.cloned.1.call-update) | async-done | bytes 10485776 | tf_op jit(solution)/shard_map/all_gather | solution.py:23
  344.6 6.4 %dynamic-slice_select_fusion = bf16[2560,1024]{1,0:T(8,128)(2,1)} fusion(bf16[5120,1024]{1,0:T(8,128)(2,1)} %all-gather.5.cloned.1.call-done, s32[]{:T(128)S(6)} %select_n.40, pred[]{:T(512)S(6)} %eq.11), kind=kLoop, calls=%fused_computation.3 | loop fusion | flops 2621440 | bytes 10485765 | tf_op jit(solution)/shard_map/jit(_where)/select_n | solution.py:10
  351.0 0.0 all-reduce.2.cloned.1.call-update
  351.0 0.0 copy-done.1
  351.0 0.6 fusion.8
  351.6 0.0 copy-done
  351.6 1.2 convert_divide_fusion
  352.8 187.3 %all-reduce.2.cloned.1.call-done = bf16[2560,1024]{1,0:T(8,128)(2,1)} async-done(((bf16[2560,1024]{1,0:T(8,128)(2,1)}), bf16[2560,1024]{1,0:T(8,128)(2,1)}) %all-reduce.2.cloned.1.call-update) | async-done | bytes 5242896 | tf_op jit(solution)/shard_map/psum | solution.py:11
  540.1 40.5 %convert_add_fusion = f32[2560,5120]{1,0:T(8,128)} fusion(bf16[2560,5120]{1,0:T(8,128)(2,1)} %param.4, bf16[5120,1024]{1,0:T(8,128)(2,1)} %all-gather.5.cloned.1.call-done, bf16[2560,1024]{1,0:T(8,128)(2,1)} %all-reduce.2.cloned.1.call-done, f32[1024]{0:T(1024)S(1)} %convert_divide_fusion), kind=kOutput, calls=%fused_computation | convolution fusion | flops 26877624320 | bytes 94375936 | tf_op jit(solution)/shard_map/dot_general | solution.py:31
Async XLA Ops:
  6.5 102.8 %all-gather.3.cloned.1.call-start = ((), (), s32[]{:S(2)}) async-start(), calls=%async_computation.1 | async-start | bytes 6553600 | tf_op jit(solution)/shard_map/all_gather | solution.py:16
  7.3 270.9 %reduce-scatter.2.cloned.1.call-start = ((), (), s32[]{:S(2)}) async-start(), calls=%async_computation.2 | async-start | bytes 23592960 | tf_op jit(solution)/shard_map/reduce_scatter | solution.py:20
  143.8 207.2 %copy-start.1 = (s32[2]{0:T(128)S(1)}, s32[2]{0:T(128)}, u32[]{:S(2)}) copy-start(s32[2]{0:T(128)} %param.7) | copy-start | bytes 28
  143.8 207.7 %copy-start = (f32[1024]{0:T(1024)S(1)}, f32[1024]{0:T(1024)}, u32[]{:S(2)}) copy-start(f32[1024]{0:T(1024)} %param.6) | copy-start | bytes 12292
  143.8 200.7 %all-gather.5.cloned.1.call-start = ((), (), s32[]{:S(2)}) async-start(), calls=%async_computation.3 | async-start | bytes 11796480 | tf_op jit(solution)/shard_map/all_gather | solution.py:23
  281.1 258.9 %all-reduce.2.cloned.1.call-start = ((), (), s32[]{:S(2)}) async-start(), calls=%async_computation.4 | async-start | bytes 10485760 | tf_op jit(solution)/shard_map/psum | solution.py:11
Sparse Core Ops, SparseCore 0:
  8.9 100.3 all-gather.2
  143.9 134.1 reduce-scatter.1
  281.3 63.2 all-gather.4
  351.1 188.9 all-reduce.1
where the time goes:
time: 587 us
  waiting for transfers between devices  488 us (83%)
  matrix products  75 us (13%)
  between operations  13.2 us (2%)
  other arithmetic  10.6 us (2%)
    psum x1, waiting for transfers between devices, spread(): return lax.psum(block, axis)  187 us
    reduce_scatter x1, waiting for transfers between devices, shards(): lax.psum_scatter(partial_value, 'row', scatter_dimension=0, tiled=True)  134 us
    all_gather x1, waiting for transfers between devices, shards(): animals = lax.all_gather(core_noncore, 'col', axis=1, tiled=True)  102 us
    all_gather x1, waiting for transfers between devices, shards(): column_panel = lax.all_gather(share, 'row', axis=0, tiled=True)  63.2 us
    dot_general x1, matrix products, shards(): lax.dot_general(scaled, column_panel, (((1,), (1,)), ((), ())), preferred...  40.5 us
    dot_general x1, matrix products, shards(): lax.dot_general(core_inverse, animals, (((0,), (0,)), ((), ())), preferre...  34.4 us
  transfers between devices with their start and end apart: 4, of which 4 were waited for; matrix products, arithmetic and copies ran while one was open for 0% of the time, Pallas kernels for 0%

commit v1 on v0

v1 whole, which is shorter than its diff:
```python
import functools

import jax
import jax.numpy as jnp
from jax import lax
from jax.experimental import pallas as pl
from jax.experimental.pallas import tpu as pltpu
from jax.sharding import PartitionSpec as P

GROUP = 512
BF16 = jnp.bfloat16
F32 = jnp.float32


VMEM = 60 * 2**20
PIECES = 1


def after(value, *others):
    return lax.optimization_barrier((value, *others))[0]


def largest_block(size, most):
    return max([b for b in range(16, most + 1, 16) if size % b == 0], default=size)


def send_kernel(ids, turned, core, out):
    out[...] = jnp.dot(turned[...], core[...], preferred_element_type=F32).astype(BF16)


def own_kernel(count, ids, turned, core, *refs):
    others, own, outs = refs[: -count - 1], refs[-count - 1], refs[-count:]
    i = pl.program_id(0)
    value = jnp.dot(turned[...], core[...], preferred_element_type=F32)
    for other in others:
        value = value + other[...].astype(F32)

    @pl.when(i == ids[0])
    def _():
        own[...] = value
        for out in outs:
            out[...] = jnp.zeros_like(out)

    @pl.when(i != ids[0])
    def _():
        depth = outs[0].shape[0]
        for n, out in enumerate(outs):
            out[...] = value[n * depth : (n + 1) * depth].astype(BF16)


def stage(kernel, ids, turned, core, mask, others, col_size, twins, out_specs, out_shape):
    slots, rows = turned.shape
    part = core.shape[1] // twins // col_size
    return pl.pallas_call(
        kernel,
        grid_spec=pltpu.PrefetchScalarGridSpec(
            num_scalar_prefetch=1,
            grid=(col_size,),
            in_specs=[
                pl.BlockSpec((slots, rows), lambda j, ids: (0, 0)),
                pl.BlockSpec(
                    (rows, part), lambda j, ids: (0, (ids[1] ^ mask) * col_size + j)
                ),
            ]
            + [pl.BlockSpec((slots, part), lambda j, ids: (0, j))] * len(others),
            out_specs=out_specs,
        ),
        out_shape=out_shape,
        cost_estimate=pl.CostEstimate(
            flops=2 * rows * slots * part * col_size,
            bytes_accessed=2 * rows * (part * col_size + slots),
            transcendentals=0,
        ),
        compiler_params=pltpu.CompilerParams(vmem_limit_bytes=VMEM),
        name="own" if others else "send",
    )(ids, turned, core, *others)


def send(ids, turned, core, col_size, twins, flip):
    slots = turned.shape[0]
    part = core.shape[1] // twins // col_size
    result = []
    for mask in range(1, twins):
        if part % 128:
            value = jnp.dot(turned, core, preferred_element_type=F32)
            value = value.reshape(slots, twins, col_size * part)
            value = lax.dynamic_index_in_dim(value, ids[1] ^ mask, 1, keepdims=False)
            value = value.astype(BF16)
        else:
            value = stage(
                send_kernel,
                ids,
                turned,
                core,
                mask,
                [],
                col_size,
                twins,
                pl.BlockSpec((slots, part), lambda j, ids: (0, j)),
                jax.ShapeDtypeStruct((slots, part * col_size), BF16),
            )
        result.append((value, flip(value, mask)))
    return result


def project(ids, turned, core, others, col_size, twins):
    others = [x[1] if isinstance(x, tuple) else x for x in others]
    slots = turned.shape[0]
    part = core.shape[1] // twins // col_size
    k, t = ids[0], ids[1]
    if part % 128:
        value = jnp.dot(turned, core, preferred_element_type=F32)
        value = value.reshape(slots, twins, col_size * part)
        total = lax.dynamic_index_in_dim(value, t, 1, keepdims=False)
        for other in others:
            total = total + other.astype(F32)
        total = jnp.moveaxis(total.reshape(slots, col_size, part), 1, 0)
        own = lax.dynamic_index_in_dim(total, k, 0, keepdims=False)
        mine = jnp.arange(col_size)[:, None, None] == k
        total = jnp.where(mine, 0, total).astype(BF16)
        return own, jnp.split(total, PIECES, axis=1)
    own, *outs = stage(
        functools.partial(own_kernel, PIECES),
        ids,
        turned,
        core,
        0,
        others,
        col_size,
        twins,
        [
            pl.BlockSpec((slots, part), lambda j, ids: (0, 0)),
        ]
        + [pl.BlockSpec((None, slots // PIECES, part), lambda j, ids: (j, 0, 0))] * PIECES,
        [
            jax.ShapeDtypeStruct((slots, part), F32),
        ]
        + [jax.ShapeDtypeStruct((col_size, slots // PIECES, part), BF16)] * PIECES,
    )
    return own, outs


def finish_kernel(own, *refs):
    others, out = refs[:-1], refs[-1]
    depth = others[0].shape[1]
    for n, other in enumerate(others):
        rows = slice(n * depth, (n + 1) * depth)
        value = own[rows, :]
        for i in range(other.shape[0]):
            value = value + other[i].astype(F32)
        out[rows, :] = value.astype(BF16)


def finish(own, others):
    size = sum(x.size for x in others)
    return pl.pallas_call(
        finish_kernel,
        out_shape=jax.ShapeDtypeStruct(own.shape, BF16),
        cost_estimate=pl.CostEstimate(
            flops=size, bytes_accessed=6 * own.size + 2 * size, transcendentals=0
        ),
        compiler_params=pltpu.CompilerParams(vmem_limit_bytes=VMEM),
        name="finish",
    )(own, *others)


def update_kernel(twins, spans, ids, live, *refs):
    masks = len(refs) - 7
    pieces, (residual, base, source, out) = refs[:masks], refs[masks:-3]
    scaled, panel, sems = refs[-3:]
    depth, part = pieces[0].shape
    block = out.shape[0]

    @pl.when(pl.program_id(0) == 0)
    def _():
        count, _, cols = source.shape
        copies = []
        for r in range(count):
            place = r % twins * (count // twins) + r // twins if count > 1 else 0
            copies.append(
                pltpu.make_async_copy(
                    source.at[r], panel.at[:, pl.ds(place * cols, cols)], sems.at[r]
                )
            )
        for copy in copies:
            copy.start()
        slot = lax.broadcasted_iota(jnp.int32, residual.shape, 1)
        limit = jnp.where(slot < GROUP, live[0], live[1])
        inside = jnp.where(slot < GROUP, slot, slot - GROUP)
        weight = (inside < limit).astype(F32) / residual[...]
        weight = jnp.concatenate([weight[:, a:b] for a, b in spans], axis=1)
        for p, piece in enumerate(pieces):
            value = piece[...].T.astype(F32) * weight
            scaled[p * part : (p + 1) * part, :] = value.astype(BF16)
        for copy in copies:
            copy.wait()

    rows = pl.ds(pl.multiple_of(pl.program_id(0) * block, block), block)
    out[...] = base[...].astype(F32) + jnp.dot(
        scaled[rows, :], panel[...], preferred_element_type=F32
    )


def update(base, pieces, masks, spans, residual, panel, ids, live, twins):
    first, step = masks[0], masks[1] - masks[0]
    depth, part = pieces[0].shape
    rows, cols = base.shape
    block = largest_block(part, 128)
    steps = part // block

    def index(i, ids, live):
        place = ids[0] ^ ids[2] ^ (first + step * (i // steps))
        return place * steps + i % steps, 0

    tile = pl.BlockSpec((block, cols), index)
    operands = [*pieces, residual]
    in_specs = [pl.BlockSpec(x.shape, lambda i, *_: (0, 0)) for x in operands]
    return pl.pallas_call(
        functools.partial(update_kernel, twins, spans),
        grid_spec=pltpu.PrefetchScalarGridSpec(
            num_scalar_prefetch=2,
            grid=(len(masks) * steps,),
            in_specs=[*in_specs, tile, pl.BlockSpec(memory_space=pl.ANY)],
            out_specs=tile,
            scratch_shapes=[
                pltpu.VMEM((len(masks) * part, depth), BF16),
                pltpu.VMEM((depth, cols), BF16),
                pltpu.SemaphoreType.DMA((panel.shape[0],)),
            ],
        ),
        out_shape=jax.ShapeDtypeStruct((rows, cols), F32),
        input_output_aliases={2 + len(operands): 0} if base.dtype == F32 else {},
        cost_estimate=pl.CostEstimate(
            flops=2 * len(masks) * part * cols * depth,
            bytes_accessed=len(masks) * part * cols * 6 + 2 * cols * depth,
            transcendentals=0,
        ),
        compiler_params=pltpu.CompilerParams(vmem_limit_bytes=VMEM),
        name="update",
    )(ids, live, *operands, base, panel)


def shards(row_size, col_size, core_inverse, core_noncore, residual, group_live):
    rows, cols = core_inverse.shape
    width = core_noncore.shape[1]
    twins = row_size // col_size
    part = rows // col_size
    row, z = lax.axis_index("row"), lax.axis_index("col")
    k, t = row // twins, row % twins
    ids = jnp.stack([k, t, z]).astype(jnp.int32)

    def flip(value, mask):
        return lax.ppermute(value, "row", [(r, r ^ mask) for r in range(row_size)])

    def cross(value, mask):
        pairs = []
        for r in range(row_size):
            for c in range(col_size):
                to_row = c * twins + r % twins
                to_col = (r // twins) ^ c ^ mask
                pairs.append((r * col_size + c, to_row * col_size + to_col))
        return lax.ppermute(value, ("row", "col"), pairs)

    def exchange(value):
        plane = [
            [c * twins + twin for c in range(col_size)] for twin in range(twins)
        ]
        return lax.all_to_all(value, "row", 0, 0, axis_index_groups=plane)

    half = width // 2
    batches = [list(range(0, col_size, 2)), list(range(1, col_size, 2))]
    turned = core_noncore.T
    animals = [
        lax.all_gather(turned[i * half : (i + 1) * half], "col", axis=0, tiled=True)
        for i in range(2)
    ]

    sent = send(ids, animals[0], core_inverse, col_size, twins, flip)
    own, others = project(ids, animals[0], core_inverse, sent, col_size, twins)
    others = [exchange(x) for x in others]
    sent = send(ids, animals[1], core_inverse, col_size, twins, flip)
    groups = [finish(after(own, *[x[0] for x in sent]), others)]
    first = after(groups[0], animals[1])
    crossed = [[cross(first, mask)] for mask in range(col_size)]
    own, others = project(
        ids, animals[1], core_inverse, [x[1] for x in sent], col_size, twins
    )
    others = [exchange(x) for x in others]
    groups.append(finish(after(own, *[x[0] for x in crossed]), others))
    for mask in range(col_size):
        crossed[mask].append(cross(groups[1], mask))
    panels = []
    for group in groups:
        panel = lax.all_gather(group, "row", axis=0)
        if part % 128:
            panel = panel.reshape(col_size, twins, *group.shape)
            panel = jnp.transpose(panel, (2, 1, 0, 3)).reshape(1, -1, cols)
        panels.append(panel)

    out = core_inverse
    for number, batch in ((0, list(range(col_size))), (1, batches[0]), (1, batches[1])):
        starts = [q * width + number * half for q in range(col_size)]
        out = update(
            out,
            [crossed[mask][number] for mask in batch],
            batch,
            [(a, a + half) for a in starts],
            residual[None, :],
            panels[number],
            ids,
            group_live,
            twins,
        )
    return out


def solution(mesh):
    return jax.shard_map(
        functools.partial(shards, mesh.shape["row"], mesh.shape["col"]),
        mesh=mesh,
        in_specs=(P("row", "col"), P("row", "col"), P(), P()),
        out_specs=P("row", "col"),
        check_vma=False,
    )
```

time: 587 us -> 404 us (0.69); the launches traced: 587 us -> 398 us
  waiting for transfers between devices: 488 us -> 175 us
  Pallas kernels: 0 us -> 154 us
  matrix products: 75 us -> 0 us
  starting transfers between devices: 0.31 us -> 44.1 us
  local copies, waits for them, and re-layouts: 0.57 us -> 11.3 us
  other arithmetic: 10.6 us -> 0.58 us
    psum x1 -> x0, waiting for transfers between devices: 187 us -> none  [spread(): return lax.psum(block, axis)]
    pallas_call x0 -> x9, Pallas kernels: none -> 154 us  [the longest x3 92.1 us: update(): pl.pallas_call(functools.partial(update_kernel, twins, spans), grid_spec=...]
    reduce_scatter x1 -> x0, waiting for transfers between devices: 134 us -> none  [shards(): lax.psum_scatter(partial_value, 'row', scatter_dimension=0, tiled=True)]
    dot_general x2 -> x0, matrix products: 75 us -> none  [the longest x1 40.5 us: shards(): lax.dot_general(scaled, column_panel, (((1,), (1,)), ((), ())), preferred...]
    ppermute x0 -> x10, waiting for transfers between devices: none -> 64 us  [the longest x8 53.8 us: cross(): return lax.ppermute(value, ('row', 'col'), pairs)]
    all_gather x2 -> x4, waiting for transfers between devices: 165 us -> 109 us  [the longest x2 86.2 us: shards(): lax.all_gather(turned[i * half:(i + 1) * half], 'col', axis=0, tiled=True)]
    ppermute x0 -> x10, starting transfers between devices: none -> 36.5 us  [the longest x8 36.4 us: cross(): return lax.ppermute(value, ('row', 'col'), pairs)]
    unnamed x4 -> x27, local copies, waits for them, and re-layouts: 0.01 us -> 10.1 us
  transfers between devices with their start and end apart: 4 -> 16, of which waited for: 4 -> 9; matrix products, arithmetic and copies ran while one was open for 0% -> 0% of each run, Pallas kernels for 0% -> 24%
where the time goes in v1:
time: 404 us; the launch traced here: 398 us
  waiting for transfers between devices  175 us (43%)
  Pallas kernels  154 us (38%)
  starting transfers between devices  44.1 us (11%)
  between operations  13.4 us (3%)
  local copies, waits for them, and re-layouts  11.3 us (3%)
    pallas_call x3, Pallas kernels, update(): pl.pallas_call(functools.partial(update_kernel, twins, spans), grid_spec=...  92.1 us
    all_gather x2, waiting for transfers between devices, shards(): lax.all_gather(turned[i * half:(i + 1) * half], 'col', axis=0, tiled=True)  86.2 us
    pallas_call x4, Pallas kernels, stage(): pl.pallas_call(kernel, grid_spec=pltpu.PrefetchScalarGridSpec(num_scalar_...  54.8 us
    ppermute x8, waiting for transfers between devices, cross(): return lax.ppermute(value, ('row', 'col'), pairs)  53.8 us
    ppermute x8, starting transfers between devices, cross(): return lax.ppermute(value, ('row', 'col'), pairs)  36.4 us
    all_gather x2, waiting for transfers between devices, shards(): panel = lax.all_gather(group, 'row', axis=0)  22.9 us
    ppermute x2, waiting for transfers between devices, flip(): return lax.ppermute(value, 'row', [(r, r ^ mask) for r in range(row_size)])  10.2 us
    unnamed x27, local copies, waits for them, and re-layouts  10.1 us
  transfers between devices with their start and end apart: 16, of which 9 were waited for; matrix products, arithmetic and copies ran while one was open for 0% of the time, Pallas kernels for 24%

profile of v1, /device:TPU:0, one launch (start us, length us, event | category | flops | bytes accessed | tf_op | source)
XLA Modules:
  0.0 398.2 jit_solution(12362888076585364911)
XLA Ops:
  6.5 1.6 copy.7
  8.1 1.1 fusion
  9.3 0.0 all-gather.9.cloned.1.call-update
  9.3 0.0 all-gather.7.cloned.1.call-start
  9.4 0.6 pad_add_fusion.ids
  9.9 57.0 %all-gather.9.cloned.1.call-done.turned = bf16[512,2560]{1,0:T(8,128)(2,1)} async-done(((bf16[128,2560]{1,0:T(8,128)(2,1)}), bf16[512,2560]{1,0:T(8,128)(2,1)}) %all-gather.9.cloned.1.call-update) | async-done | bytes 2621456 | tf_op jit(solution)/shard_map/all_gather | solution.py:274
  67.0 13.1 %send.3 = bf16[512,2560]{1,0:T(8,128)(2,1)} custom-call(s32[3]{0:T(128)} %pad_add_fusion.ids, bf16[512,2560]{1,0:T(8,128)(2,1)} %all-gather.9.cloned.1.call-done.turned, bf16[2560,5120]{1,0:T(8,128)(2,1)} %refs_5_.1), custom_call_target="tpu_custom_call" | custom-call | flops 6710886400 | bytes 15728640 | tf_op jit(solution)/shard_map/send/pallas_call | solution.py:54
  80.1 0.0 collective-permute-start.1
  80.1 0.0 all-gather.7.cloned.1.call-update
  80.1 5.1 %collective-permute-done.1.refs_0_ = bf16[512,2560]{1,0:T(8,128)(2,1)S(1)} collective-permute-done((bf16[512,2560]{1,0:T(8,128)(2,1)}, bf16[512,2560]{1,0:T(8,128)(2,1)S(1)}, u32[]{:S(2)}, u32[]{:S(2)}) %collective-permute-start.1) | collective-permute-done | bytes 2621472 | tf_op jit(solution)/shard_map/ppermute | solution.py:253
  85.2 1.5 copy-done.2
  86.7 14.4 %own.3 = (f32[512,640]{1,0:T(8,128)}, bf16[4,512,640]{2,1,0:T(8,128)(2,1)}) custom-call(s32[3]{0:T(128)} %pad_add_fusion.ids, bf16[512,2560]{1,0:T(8,128)(2,1)} %all-gather.9.cloned.1.call-done.turned, bf16[2560,5120]{1,0:T(8,128)(2,1)} %refs_5_.1, bf16[512,2560]{1,0:T(8,128)(2,1)} %copy-done.2), custom_call_target="tpu_custom_call" | custom-call | flops 6710886400 | bytes 15728640 | tf_op jit(solution)/shard_map/own/pallas_call | solution.py:54
  101.1 3.7 all-to-all-start
  104.8 0.0 all-gather.11.cloned.1.call-start
  104.8 29.1 %all-gather.7.cloned.1.call-done.turned = bf16[512,2560]{1,0:T(8,128)(2,1)} async-done(((bf16[128,2560]{1,0:T(8,128)(2,1)}), bf16[512,2560]{1,0:T(8,128)(2,1)}) %all-gather.7.cloned.1.call-update) | async-done | bytes 2621456 | tf_op jit(solution)/shard_map/all_gather | solution.py:274
  134.0 13.1 %send.2 = bf16[512,2560]{1,0:T(8,128)(2,1)} custom-call(s32[3]{0:T(128)} %pad_add_fusion.ids, bf16[512,2560]{1,0:T(8,128)(2,1)} %all-gather.7.cloned.1.call-done.turned, bf16[2560,5120]{1,0:T(8,128)(2,1)} %refs_5_.1), custom_call_target="tpu_custom_call" | custom-call | flops 6710886400 | bytes 15728640 | tf_op jit(solution)/shard_map/send/pallas_call | solution.py:54
  147.1 0.0 all-to-all-done.refs_0_
  147.1 1.5 copy-done.1
  148.6 3.4 finish.2
  152.0 0.0 all-gather.11.cloned.1.call-update
  152.0 0.1 collective-permute-start
  152.1 5.1 %collective-permute-done.refs_0_ = bf16[512,2560]{1,0:T(8,128)(2,1)S(1)} collective-permute-done((bf16[512,2560]{1,0:T(8,128)(2,1)}, bf16[512,2560]{1,0:T(8,128)(2,1)S(1)}, u32[]{:S(2)}, u32[]{:S(2)}) %collective-permute-start) | collective-permute-done | bytes 2621472 | tf_op jit(solution)/shard_map/ppermute | solution.py:253
  157.2 1.5 copy-done.3
  158.7 14.1 %own.2 = (f32[512,640]{1,0:T(8,128)}, bf16[4,512,640]{2,1,0:T(8,128)(2,1)}) custom-call(s32[3]{0:T(128)} %pad_add_fusion.ids, bf16[512,2560]{1,0:T(8,128)(2,1)} %all-gather.7.cloned.1.call-done.turned, bf16[2560,5120]{1,0:T(8,128)(2,1)} %refs_5_.1, bf16[512,2560]{1,0:T(8,128)(2,1)} %copy-done.3), custom_call_target="tpu_custom_call" | custom-call | flops 6710886400 | bytes 15728640 | tf_op jit(solution)/shard_map/own/pallas_call | solution.py:54
  172.9 3.9 all-to-all-start.1
  176.8 0.7 collective-permute-start.2
  177.5 5.2 %collective-permute-start.3 = (bf16[512,640]{1,0:T(8,128)(2,1)S(1)}, bf16[512,640]{1,0:T(8,128)(2,1)S(1)}, u32[]{:S(2)}, u32[]{:S(2)}) collective-permute-start(bf16[512,640]{1,0:T(8,128)(2,1)S(1)} %copy-done.4), channel_id=1, source_target_pairs={{0,1},{1,8},{2,19},{3,26},{4,5},{5,12},{6,23},{7,30},{8,0},{9,9},{... | collective-permute-start | bytes 1966088 | tf_op jit(solution)/shard_map/ppermute | solution.py:262
  182.6 5.2 %collective-permute-start.4 = (bf16[512,640]{1,0:T(8,128)(2,1)S(1)}, bf16[512,640]{1,0:T(8,128)(2,1)S(1)}, u32[]{:S(2)}, u32[]{:S(2)}) collective-permute-start(bf16[512,640]{1,0:T(8,128)(2,1)S(1)} %copy-done.4), channel_id=1, source_target_pairs={{0,2},{1,11},{2,16},{3,25},{4,6},{5,15},{6,20},{7,29},{8,3},{9,10}... | collective-permute-start | bytes 1966088 | tf_op jit(solution)/shard_map/ppermute | solution.py:262
  187.8 5.8 %collective-permute-start.5 = (bf16[512,640]{1,0:T(8,128)(2,1)S(1)}, bf16[512,640]{1,0:T(8,128)(2,1)S(1)}, u32[]{:S(2)}, u32[]{:S(2)}) collective-permute-start(bf16[512,640]{1,0:T(8,128)(2,1)S(1)} %copy-done.4), channel_id=1, source_target_pairs={{0,3},{1,10},{2,17},{3,24},{4,7},{5,14},{6,21},{7,28},{8,2},{9,11}... | collective-permute-start | bytes 1966088 | tf_op jit(solution)/shard_map/ppermute | solution.py:262
  193.7 50.6 %collective-permute-done.3.refs_1_ = bf16[512,640]{1,0:T(8,128)(2,1)S(1)} collective-permute-done((bf16[512,640]{1,0:T(8,128)(2,1)S(1)}, bf16[512,640]{1,0:T(8,128)(2,1)S(1)}, u32[]{:S(2)}, u32[]{:S(2)}) %collective-permute-start.3) | collective-permute-done | bytes 655392 | tf_op jit(solution)/shard_map/ppermute | solution.py:262
  244.3 1.0 collective-permute-done.4.refs_2_
  245.3 2.2 collective-permute-done.5.refs_3_
  247.4 0.8 copy-done.8
  248.3 2.1 all-to-all-done.1.refs_0_
  250.4 1.5 copy-done
  251.9 3.4 finish.3
  255.3 0.0 all-gather.13.cloned.1.call-update
  255.3 1.7 collective-permute-start.8
  257.0 10.5 %collective-permute-start.9 = (bf16[512,640]{1,0:T(8,128)(2,1)}, bf16[512,640]{1,0:T(8,128)(2,1)S(1)}, u32[]{:S(2)}, u32[]{:S(2)}) collective-permute-start(bf16[512,640]{1,0:T(8,128)(2,1)} %finish.3), channel_id=1, source_target_pairs={{0,2},{1,11},{2,16},{3,25},{4,6},{5,15},{6,20},{7,29},{8,3},{9,10}... | collective-permute-start | bytes 1966088 | tf_op jit(solution)/shard_map/ppermute | solution.py:262
  267.6 2.3 collective-permute-start.6
  269.9 4.9 %collective-permute-start.7 = (bf16[512,640]{1,0:T(8,128)(2,1)}, bf16[512,640]{1,0:T(8,128)(2,1)S(1)}, u32[]{:S(2)}, u32[]{:S(2)}) collective-permute-start(bf16[512,640]{1,0:T(8,128)(2,1)} %finish.3), channel_id=1, source_target_pairs={{0,3},{1,10},{2,17},{3,24},{4,7},{5,14},{6,21},{7,28},{8,2},{9,11}... | collective-permute-start | bytes 1966088 | tf_op jit(solution)/shard_map/ppermute | solution.py:262
  274.9 0.0 all-gather.11.cloned.1.call-done
  274.9 38.5 %update.3.refs_3_ = f32[2560,5120]{1,0:T(8,128)} custom-call(s32[3]{0:T(128)} %pad_add_fusion.ids, s32[2]{0:T(128)} %live.5, bf16[512,640]{1,0:T(8,128)(2,1)} %copy-done.5, bf16[512,640]{1,0:T(8,128)(2,1)} %copy-done.6, bf16[512,640]{1,0:T(8,128)(2,1)} %copy-done.7, bf16[512,640]{1,0:T(8,128)(2,1)} %copy-done.8, f32[1,1024]{1,0:T(1,128)} %bitcast.11, ...), custom_call_target="tpu_custom_call" | custom-call | flops 13421772800 | bytes 83886080 | tf_op jit(solution)/shard_map/update/pallas_call | solution.py:218
  313.4 22.9 %all-gather.13.cloned.1.call-done = bf16[4096,640]{1,0:T(8,128)(2,1)} async-done(((bf16[512,640]{1,0:T(8,128)(2,1)}), bf16[4096,640]{1,0:T(8,128)(2,1)}) %all-gather.13.cloned.1.call-update) | async-done | bytes 5242896 | tf_op jit(solution)/shard_map/all_gather | solution.py:294
  336.3 26.8 %update.4.refs_3_ = f32[2560,5120]{1,0:T(8,128)} custom-call(s32[3]{0:T(128)} %pad_add_fusion.ids, s32[2]{0:T(128)} %live.5, bf16[512,640]{1,0:T(8,128)(2,1)} %copy-done.11, bf16[512,640]{1,0:T(8,128)(2,1)} %copy-done.12, f32[1,1024]{1,0:T(1,128)} %bitcast.12, f32[2560,5120]{1,0:T(8,128)} %update.3.refs_3_, ...), custom_call_target="tpu_custom_call", output_to_operand_aliasing={{}: (5, {})} | custom-call | flops 6710886400 | bytes 44564480 | tf_op jit(solution)/shard_map/update/pallas_call | solution.py:218
  363.1 0.8 copy-done.9
  364.0 0.8 copy-done.10
  364.8 26.8 %update.5 = f32[2560,5120]{1,0:T(8,128)} custom-call(s32[3]{0:T(128)} %pad_add_fusion.ids, s32[2]{0:T(128)} %live.5, bf16[512,640]{1,0:T(8,128)(2,1)} %copy-done.9, bf16[512,640]{1,0:T(8,128)(2,1)} %copy-done.10, f32[1,1024]{1,0:T(1,128)} %bitcast.13, f32[2560,5120]{1,0:T(8,128)} %update.4.refs_3_, ...), custom_call_target="tpu_custom_call", output_to_operand_aliasing={{}: (5, {})} | custom-call | flops 6710886400 | bytes 44564480 | tf_op jit(solution)/shard_map/update/pallas_call | solution.py:218
  (26 shorter events, 0.1 us)
Async XLA Ops:
  6.5 60.4 %all-gather.9.cloned.1.call-start = ((), (), s32[]{:S(2)}) async-start(), calls=%async_computation.3 | async-start | bytes 3276800 | tf_op jit(solution)/shard_map/all_gather | solution.py:274
  9.3 124.7 %all-gather.7.cloned.1.call-start = ((), (), s32[]{:S(2)}) async-start(), calls=%async_computation.2 | async-start | bytes 3276800 | tf_op jit(solution)/shard_map/all_gather | solution.py:274
  80.1 5.1 %collective-permute-start.1 = (bf16[512,2560]{1,0:T(8,128)(2,1)}, bf16[512,2560]{1,0:T(8,128)(2,1)S(1)}, u32[]{:S(2)}, u32[]{:S(2)}) collective-permute-start(bf16[512,2560]{1,0:T(8,128)(2,1)} %send.3), channel_id=1, source_target_pairs={{0,4},{4,0},{8,12},{12,8},{16,20},{20,16},{24,28},{28,24},{1,5},{5... | collective-permute-start | bytes 7864328 | tf_op jit(solution)/shard_map/ppermute | solution.py:253
  85.2 1.5 copy-start.2
  101.1 46.0 %all-to-all-start = ((bf16[4,512,640]{2,1,0:T(8,128)(2,1)}), bf16[4,512,640]{2,1,0:T(8,128)(2,1)S(1)}, u32[]{:S(2)}, u32[]{:S(2)}) async-start(bf16[4,512,640]{2,1,0:T(8,128)(2,1)} %get-tuple-element.15), calls=%async_computation | async-start | bytes 5242880 | tf_op jit(solution)/shard_map/all_to_all | solution.py:268
  104.8 170.1 %all-gather.11.cloned.1.call-start = ((), (), s32[]{:S(2)}) async-start(), calls=%async_computation.4 | async-start | bytes 5898240 | tf_op jit(solution)/shard_map/all_gather | solution.py:294
  147.1 1.5 copy-start.1
  152.0 5.2 %collective-permute-start = (bf16[512,2560]{1,0:T(8,128)(2,1)}, bf16[512,2560]{1,0:T(8,128)(2,1)S(1)}, u32[]{:S(2)}, u32[]{:S(2)}) collective-permute-start(bf16[512,2560]{1,0:T(8,128)(2,1)} %send.2), channel_id=1, source_target_pairs={{0,4},{4,0},{8,12},{12,8},{16,20},{20,16},{24,28},{28,24},{1,5},{5... | collective-permute-start | bytes 7864328 | tf_op jit(solution)/shard_map/ppermute | solution.py:253
  157.2 1.5 copy-start.3
  172.9 3.9 copy-start.4
  172.9 77.5 %all-to-all-start.1 = ((bf16[4,512,640]{2,1,0:T(8,128)(2,1)}), bf16[4,512,640]{2,1,0:T(8,128)(2,1)S(1)}, u32[]{:S(2)}, u32[]{:S(2)}) async-start(bf16[4,512,640]{2,1,0:T(8,128)(2,1)} %get-tuple-element.18), calls=%async_computation.1 | async-start | bytes 5242880 | tf_op jit(solution)/shard_map/all_to_all | solution.py:268
  176.8 159.5 %all-gather.13.cloned.1.call-start = ((), (), s32[]{:S(2)}) async-start(), calls=%async_computation.5 | async-start | bytes 5898240 | tf_op jit(solution)/shard_map/all_gather | solution.py:294
  176.8 16.9 %collective-permute-start.2 = (bf16[512,640]{1,0:T(8,128)(2,1)S(1)}, bf16[512,640]{1,0:T(8,128)(2,1)S(1)}, u32[]{:S(2)}, u32[]{:S(2)}) collective-permute-start(bf16[512,640]{1,0:T(8,128)(2,1)S(1)} %copy-done.4), channel_id=1, source_target_pairs={{0,0},{1,9},{2,18},{3,27},{4,4},{5,13},{6,22},{7,31},{8,1},{9,8},{... | collective-permute-start | bytes 1966088 | tf_op jit(solution)/shard_map/ppermute | solution.py:262
  177.5 66.8 %collective-permute-start.3 = (bf16[512,640]{1,0:T(8,128)(2,1)S(1)}, bf16[512,640]{1,0:T(8,128)(2,1)S(1)}, u32[]{:S(2)}, u32[]{:S(2)}) collective-permute-start(bf16[512,640]{1,0:T(8,128)(2,1)S(1)} %copy-done.4), channel_id=1, source_target_pairs={{0,1},{1,8},{2,19},{3,26},{4,5},{5,12},{6,23},{7,30},{8,0},{9,9},{... | collective-permute-start | bytes 1966088 | tf_op jit(solution)/shard_map/ppermute | solution.py:262
  182.6 62.6 %collective-permute-start.4 = (bf16[512,640]{1,0:T(8,128)(2,1)S(1)}, bf16[512,640]{1,0:T(8,128)(2,1)S(1)}, u32[]{:S(2)}, u32[]{:S(2)}) collective-permute-start(bf16[512,640]{1,0:T(8,128)(2,1)S(1)} %copy-done.4), channel_id=1, source_target_pairs={{0,2},{1,11},{2,16},{3,25},{4,6},{5,15},{6,20},{7,29},{8,3},{9,10}... | collective-permute-start | bytes 1966088 | tf_op jit(solution)/shard_map/ppermute | solution.py:262
  187.8 59.6 %collective-permute-start.5 = (bf16[512,640]{1,0:T(8,128)(2,1)S(1)}, bf16[512,640]{1,0:T(8,128)(2,1)S(1)}, u32[]{:S(2)}, u32[]{:S(2)}) collective-permute-start(bf16[512,640]{1,0:T(8,128)(2,1)S(1)} %copy-done.4), channel_id=1, source_target_pairs={{0,3},{1,10},{2,17},{3,24},{4,7},{5,14},{6,21},{7,28},{8,2},{9,11}... | collective-permute-start | bytes 1966088 | tf_op jit(solution)/shard_map/ppermute | solution.py:262
  193.7 53.8 %copy-start.5 = (bf16[512,640]{1,0:T(8,128)(2,1)}, bf16[512,640]{1,0:T(8,128)(2,1)S(1)}, u32[]{:S(2)}) copy-start(bf16[512,640]{1,0:T(8,128)(2,1)S(1)} %collective-permute-done.2.refs_0_) | copy-start | bytes 1966084
  244.3 3.2 copy-start.6
  245.3 2.2 copy-start.7
  247.4 0.8 copy-start.8
  250.4 1.5 copy-start
  255.3 58.1 %collective-permute-start.8 = (bf16[512,640]{1,0:T(8,128)(2,1)}, bf16[512,640]{1,0:T(8,128)(2,1)S(1)}, u32[]{:S(2)}, u32[]{:S(2)}) collective-permute-start(bf16[512,640]{1,0:T(8,128)(2,1)} %finish.3), channel_id=1, source_target_pairs={{0,0},{1,9},{2,18},{3,27},{4,4},{5,13},{6,22},{7,31},{8,1},{9,8},{... | collective-permute-start | bytes 1966088 | tf_op jit(solution)/shard_map/ppermute | solution.py:262
  257.0 56.3 %collective-permute-start.9 = (bf16[512,640]{1,0:T(8,128)(2,1)}, bf16[512,640]{1,0:T(8,128)(2,1)S(1)}, u32[]{:S(2)}, u32[]{:S(2)}) collective-permute-start(bf16[512,640]{1,0:T(8,128)(2,1)} %finish.3), channel_id=1, source_target_pairs={{0,2},{1,11},{2,16},{3,25},{4,6},{5,15},{6,20},{7,29},{8,3},{9,10}... | collective-permute-start | bytes 1966088 | tf_op jit(solution)/shard_map/ppermute | solution.py:262
  267.6 95.5 %collective-permute-start.6 = (bf16[512,640]{1,0:T(8,128)(2,1)}, bf16[512,640]{1,0:T(8,128)(2,1)S(1)}, u32[]{:S(2)}, u32[]{:S(2)}) collective-permute-start(bf16[512,640]{1,0:T(8,128)(2,1)} %finish.3), channel_id=1, source_target_pairs={{0,1},{1,8},{2,19},{3,26},{4,5},{5,12},{6,23},{7,30},{8,0},{9,9},{... | collective-permute-start | bytes 1966088 | tf_op jit(solution)/shard_map/ppermute | solution.py:262
  269.9 93.2 %collective-permute-start.7 = (bf16[512,640]{1,0:T(8,128)(2,1)}, bf16[512,640]{1,0:T(8,128)(2,1)S(1)}, u32[]{:S(2)}, u32[]{:S(2)}) collective-permute-start(bf16[512,640]{1,0:T(8,128)(2,1)} %finish.3), channel_id=1, source_target_pairs={{0,3},{1,10},{2,17},{3,24},{4,7},{5,14},{6,21},{7,28},{8,2},{9,11}... | collective-permute-start | bytes 1966088 | tf_op jit(solution)/shard_map/ppermute | solution.py:262
  313.4 22.9 %copy-start.11 = (bf16[512,640]{1,0:T(8,128)(2,1)}, bf16[512,640]{1,0:T(8,128)(2,1)S(1)}, u32[]{:S(2)}) copy-start(bf16[512,640]{1,0:T(8,128)(2,1)S(1)} %collective-permute-done.8.refs_0_) | copy-start | bytes 1966084
  313.4 22.9 %copy-start.12 = (bf16[512,640]{1,0:T(8,128)(2,1)}, bf16[512,640]{1,0:T(8,128)(2,1)S(1)}, u32[]{:S(2)}) copy-start(bf16[512,640]{1,0:T(8,128)(2,1)S(1)} %collective-permute-done.9.refs_1_) | copy-start | bytes 1966084
  363.1 0.9 copy-start.9
  364.0 0.8 copy-start.10
Sparse Core Ops, SparseCore 0:
  9.4 57.4 all-gather.8
  80.2 53.7 all-gather.6
  152.2 73.5 all-gather.10
  255.4 80.8 all-gather.12

commit v2 on v1

v2 whole, which is shorter than its diff:
```python
import functools

import jax
import jax.numpy as jnp
from jax import lax
from jax.experimental import pallas as pl
from jax.experimental.pallas import tpu as pltpu
from jax.sharding import PartitionSpec as P

GROUP = 512
BF16 = jnp.bfloat16
F32 = jnp.float32


VMEM = 127 * 2**19


def after(value, *others):
    return lax.optimization_barrier((value, *others))[0]


def largest_block(size, most):
    return max([b for b in range(16, most + 1, 16) if size % b == 0], default=size)


def send_kernel(ids, turned, core, out):
    out[...] = jnp.dot(turned[...], core[...], preferred_element_type=F32).astype(BF16)


def own_kernel(ids, turned, core, *refs):
    others, (own, out) = refs[:-2], refs[-2:]
    i = pl.program_id(0)
    value = jnp.dot(turned[...], core[...], preferred_element_type=F32)
    for other in others:
        value = value + other[...].astype(F32)

    @pl.when(i == ids[0])
    def _():
        own[...] = value
        out[...] = jnp.zeros_like(out)

    @pl.when(i != ids[0])
    def _():
        out[...] = value.astype(BF16)


def stage(kernel, ids, turned, core, mask, others, col_size, twins, out_specs, out_shape):
    slots, rows = turned.shape
    part = core.shape[1] // twins // col_size
    return pl.pallas_call(
        kernel,
        grid_spec=pltpu.PrefetchScalarGridSpec(
            num_scalar_prefetch=1,
            grid=(col_size,),
            in_specs=[
                pl.BlockSpec((slots, rows), lambda j, ids: (0, 0)),
                pl.BlockSpec(
                    (rows, part), lambda j, ids: (0, (ids[1] ^ mask) * col_size + j)
                ),
            ]
            + [pl.BlockSpec((slots, part), lambda j, ids: (0, j))] * len(others),
            out_specs=out_specs,
        ),
        out_shape=out_shape,
        cost_estimate=pl.CostEstimate(
            flops=2 * rows * slots * part * col_size,
            bytes_accessed=2 * rows * (part * col_size + slots),
            transcendentals=0,
        ),
        compiler_params=pltpu.CompilerParams(vmem_limit_bytes=VMEM),
        name="own" if others else "send",
    )(ids, turned, core, *others)


def send(ids, turned, core, col_size, twins, flip):
    slots = turned.shape[0]
    part = core.shape[1] // twins // col_size
    result = []
    for mask in range(1, twins):
        if part % 128:
            value = jnp.dot(turned, core, preferred_element_type=F32)
            value = value.reshape(slots, twins, col_size * part)
            value = lax.dynamic_index_in_dim(value, ids[1] ^ mask, 1, keepdims=False)
            value = value.astype(BF16)
        else:
            value = stage(
                send_kernel,
                ids,
                turned,
                core,
                mask,
                [],
                col_size,
                twins,
                pl.BlockSpec((slots, part), lambda j, ids: (0, j)),
                jax.ShapeDtypeStruct((slots, part * col_size), BF16),
            )
        result.append((value, flip(value, mask)))
    return result


def project(ids, turned, core, others, col_size, twins):
    others = [x[1] if isinstance(x, tuple) else x for x in others]
    slots = turned.shape[0]
    part = core.shape[1] // twins // col_size
    k, t = ids[0], ids[1]
    if part % 128:
        value = jnp.dot(turned, core, preferred_element_type=F32)
        value = value.reshape(slots, twins, col_size * part)
        total = lax.dynamic_index_in_dim(value, t, 1, keepdims=False)
        for other in others:
            total = total + other.astype(F32)
        total = jnp.moveaxis(total.reshape(slots, col_size, part), 1, 0)
        own = lax.dynamic_index_in_dim(total, k, 0, keepdims=False)
        mine = jnp.arange(col_size)[:, None, None] == k
        return own, jnp.where(mine, 0, total).astype(BF16)
    return stage(
        own_kernel,
        ids,
        turned,
        core,
        0,
        others,
        col_size,
        twins,
        [
            pl.BlockSpec((slots, part), lambda j, ids: (0, 0)),
            pl.BlockSpec((None, slots, part), lambda j, ids: (j, 0, 0)),
        ],
        [
            jax.ShapeDtypeStruct((slots, part), F32),
            jax.ShapeDtypeStruct((col_size, slots, part), BF16),
        ],
    )


def finish_kernel(own, others, out):
    value = own[...]
    for i in range(others.shape[0]):
        value = value + others[i].astype(F32)
    out[...] = value.astype(BF16)


def finish(own, others):
    return pl.pallas_call(
        finish_kernel,
        out_shape=jax.ShapeDtypeStruct(own.shape, BF16),
        cost_estimate=pl.CostEstimate(
            flops=others.size,
            bytes_accessed=6 * own.size + 2 * others.size,
            transcendentals=0,
        ),
        compiler_params=pltpu.CompilerParams(vmem_limit_bytes=VMEM),
        name="finish",
    )(own, others)


def update_kernel(masks, twins, spans, places, ids, live, *refs):
    halves = refs[:masks], refs[masks : 2 * masks]
    residual, core, *sources = refs[2 * masks : -4]
    out, scaled, panel, sems = refs[-4:]
    depth, part = halves[0][0].shape
    block = out.shape[0]

    @pl.when(pl.program_id(0) == 0)
    def _():
        copies = []
        for n, (first, twin) in enumerate(places):
            source = sources[n]
            count, height, cols = source.shape
            for r in range(count):
                if twin is None:
                    place = r % twins * (count // twins) + r // twins if count > 1 else 0
                    lane = place * cols
                else:
                    place = (ids[1] ^ twin) * count + (ids[0] ^ r)
                    lane = pl.multiple_of(place * cols, cols)
                copies.append(
                    pltpu.make_async_copy(
                        source.at[r],
                        panel.at[pl.ds(first, height), pl.ds(lane, cols)],
                        sems.at[len(copies)],
                    )
                )
        for copy in copies:
            copy.start()
        slot = lax.broadcasted_iota(jnp.int32, residual.shape, 1)
        limit = jnp.where(slot < GROUP, live[0], live[1])
        inside = jnp.where(slot < GROUP, slot, slot - GROUP)
        weight = (inside < limit).astype(F32) / residual[...]
        weight = jnp.concatenate([weight[:, a:b] for a, b in spans], axis=1)
        for g, pieces in enumerate(halves):
            lanes = slice(g * depth, (g + 1) * depth)
            for p, piece in enumerate(pieces):
                value = piece[...].T.astype(F32) * weight[:, lanes]
                scaled[p * part : (p + 1) * part, lanes] = value.astype(BF16)
        for copy in copies:
            copy.wait()

    rows = pl.ds(pl.multiple_of(pl.program_id(0) * block, block), block)
    out[...] = core[...].astype(F32) + jnp.dot(
        scaled[rows, :], panel[...], preferred_element_type=F32
    )


def update(core, stacked, pieces, spans, residual, panels, places, ids, live, twins):
    masks = len(pieces)
    depth, part = pieces[0].shape
    rows, cols = core.shape
    slots = residual.shape[1]
    block = largest_block(part, 320)
    steps = part // block

    def stacked_index(mask):
        return lambda i, ids, live: (ids[0] ^ ids[2] ^ mask, 0, 0)

    tile = pl.BlockSpec(
        (block, cols),
        lambda i, ids, live: ((ids[0] ^ ids[2] ^ (i // steps)) * steps + i % steps, 0),
    )
    once = pl.Buffered(1)
    in_specs = [
        pl.BlockSpec((None, depth, part), stacked_index(mask), pipeline_mode=once)
        for mask in range(masks)
    ]
    in_specs += [
        pl.BlockSpec(x.shape, lambda i, *_: (0, 0), pipeline_mode=once) for x in pieces
    ]
    in_specs += [pl.BlockSpec(residual.shape, lambda i, *_: (0, 0)), tile]
    in_specs += [pl.BlockSpec(memory_space=pl.ANY)] * len(panels)
    return pl.pallas_call(
        functools.partial(update_kernel, masks, twins, spans, places),
        grid_spec=pltpu.PrefetchScalarGridSpec(
            num_scalar_prefetch=2,
            grid=(masks * steps,),
            in_specs=in_specs,
            out_specs=tile,
            scratch_shapes=[
                pltpu.VMEM((masks * part, slots), BF16),
                pltpu.VMEM((slots, cols), BF16),
                pltpu.SemaphoreType.DMA((sum(x.shape[0] for x in panels),)),
            ],
        ),
        out_shape=jax.ShapeDtypeStruct((rows, cols), F32),
        cost_estimate=pl.CostEstimate(
            flops=2 * rows * cols * slots,
            bytes_accessed=rows * cols * 6 + 2 * cols * slots,
            transcendentals=0,
        ),
        compiler_params=pltpu.CompilerParams(vmem_limit_bytes=VMEM),
        name="update",
    )(ids, live, *[stacked] * masks, *pieces, residual, core, *panels)


def shards(row_size, col_size, core_inverse, core_noncore, residual, group_live):
    rows, cols = core_inverse.shape
    width = core_noncore.shape[1]
    twins = row_size // col_size
    part = rows // col_size
    row, z = lax.axis_index("row"), lax.axis_index("col")
    k, t = row // twins, row % twins
    ids = jnp.stack([k, t, z]).astype(jnp.int32)

    def flip(value, mask):
        return lax.ppermute(value, "row", [(r, r ^ mask) for r in range(row_size)])

    def cross(value, mask):
        pairs = []
        for r in range(row_size):
            for c in range(col_size):
                to_row = c * twins + r % twins
                to_col = (r // twins) ^ c ^ mask
                pairs.append((r * col_size + c, to_row * col_size + to_col))
        return lax.ppermute(value, ("row", "col"), pairs)

    def exchange(value):
        plane = [
            [c * twins + twin for c in range(col_size)] for twin in range(twins)
        ]
        return lax.all_to_all(value, "row", 0, 0, axis_index_groups=plane)

    half = width // 2
    turned = core_noncore.T
    animals = [
        lax.all_gather(turned[i * half : (i + 1) * half], "col", axis=0, tiled=True)
        for i in range(2)
    ]

    def gather_plane(group):
        panel = lax.all_gather(group, "row", axis=0)
        if part % 128:
            panel = panel.reshape(col_size, twins, *group.shape)
            panel = jnp.transpose(panel, (2, 1, 0, 3)).reshape(1, -1, cols)
        return panel

    sent = send(ids, animals[0], core_inverse, col_size, twins, flip)
    own, others = project(ids, animals[0], core_inverse, sent, col_size, twins)
    others = exchange(others)
    sent = send(ids, animals[1], core_inverse, col_size, twins, flip)
    first = finish(after(own, *[x[0] for x in sent]), others)
    levels = lax.all_gather(first, "col", axis=0)
    own, others = project(ids, animals[1], core_inverse, sent, col_size, twins)
    flipped, panels = [], []
    if part % 128 == 0:
        masks = [1 << bit for bit in range(col_size.bit_length() - 1)]
        near = {mask: flip(first, mask * twins) for mask in masks}
        others = after(others, *near.values())
        for mask in range(1, col_size):
            if mask in near:
                flipped.append(near[mask])
            elif mask.bit_count() == 2:
                one = mask & -mask
                cut = first.shape[0] // 2
                flipped.append(
                    jnp.concatenate(
                        [
                            flip(near[one][:cut], (mask ^ one) * twins),
                            flip(near[mask ^ one][cut:], one * twins),
                        ]
                    )
                )
            else:
                flipped.append(flip(first, mask * twins))
        held = jnp.stack([first, *flipped])
        panels = [held] + [flip(held, twin) for twin in range(1, twins)]
    second = finish(own, exchange(others))
    crossed = [cross(second, mask) for mask in range(col_size)]
    stacked = exchange(levels)
    if flipped:
        places = [(0, twin) for twin in range(twins)]
        panels.append(gather_plane(second))
        places.append((first.shape[0], None))
    else:
        panels = [gather_plane(jnp.concatenate([first, second], axis=0))]
        places = [(0, None)]

    starts = [q * width + g * half for g in range(2) for q in range(col_size)]
    return update(
        core_inverse,
        stacked,
        crossed,
        [(a, a + half) for a in starts],
        residual[None, :],
        panels,
        places,
        ids,
        group_live,
        twins,
    )


def solution(mesh):
    return jax.shard_map(
        functools.partial(shards, mesh.shape["row"], mesh.shape["col"]),
        mesh=mesh,
        in_specs=(P("row", "col"), P("row", "col"), P(), P()),
        out_specs=P("row", "col"),
        check_vma=False,
    )
```

time: 404 us -> 347 us (0.86)
  Pallas kernels: 154 us -> 104 us
  blocking collectives: 0 us -> 35.3 us
  starting transfers between devices: 44.1 us -> 22 us
  waiting for transfers between devices: 175 us -> 156 us
    pallas_call x3 -> x1, Pallas kernels: 92.1 us -> 42.6 us  [update(): pl.pallas_call(functools.partial(update_kernel, masks, twins, spans, plac...]
    all_to_all x0 -> x1, blocking collectives: none -> 35.3 us  [exchange(): return lax.all_to_all(value, 'row', 0, 0, axis_index_groups=plane)]
    ppermute x8 -> x4, starting transfers between devices: 36.4 us -> 8.21 us  [cross(): return lax.ppermute(value, ('row', 'col'), pairs)]
    all_gather x2, waiting for transfers between devices: 22.9 us -> 0.02 us  [the longest x1 0.02 us: shards(): levels = lax.all_gather(first, 'col', axis=0)]
    all_gather x2, waiting for transfers between devices: 86.2 us -> 74.1 us  [shards(): lax.all_gather(turned[i * half:(i + 1) * half], 'col', axis=0, tiled=True)]
    ppermute x2 -> x7, waiting for transfers between devices: 10.2 us -> 19.2 us  [flip(): return lax.ppermute(value, 'row', [(r, r ^ mask) for r in range(row_size)])]
    ppermute x8 -> x4, waiting for transfers between devices: 53.8 us -> 62.1 us  [cross(): return lax.ppermute(value, ('row', 'col'), pairs)]
    unnamed x27 -> x15, local copies, waits for them, and re-layouts: 10.1 us -> 5.15 us
  transfers between devices with their start and end apart: 16 -> 17, of which waited for: 9 -> 9; matrix products, arithmetic and copies ran while one was open for 0% -> 1% of each run, Pallas kernels for 24% -> 10%
where the time goes in v2:
time: 347 us; the launch traced here: 342 us
  waiting for transfers between devices  156 us (45%)
  Pallas kernels  104 us (30%)
  blocking collectives  35.3 us (10%)
  starting transfers between devices  22 us (6%)
  between operations  13.3 us (4%)
  local copies, waits for them, and re-layouts  8.35 us (2%)
    all_gather x2, waiting for transfers between devices, shards(): lax.all_gather(turned[i * half:(i + 1) * half], 'col', axis=0, tiled=True)  74.1 us
    ppermute x4, waiting for transfers between devices, cross(): return lax.ppermute(value, ('row', 'col'), pairs)  62.1 us
    pallas_call x4, Pallas kernels, stage(): pl.pallas_call(kernel, grid_spec=pltpu.PrefetchScalarGridSpec(num_scalar_...  55.2 us
    pallas_call x1, Pallas kernels, update(): pl.pallas_call(functools.partial(update_kernel, masks, twins, spans, plac...  42.6 us
    all_to_all x1, blocking collectives, exchange(): return lax.all_to_all(value, 'row', 0, 0, axis_index_groups=plane)  35.3 us
    ppermute x7, waiting for transfers between devices, flip(): return lax.ppermute(value, 'row', [(r, r ^ mask) for r in range(row_size)])  19.2 us
    all_to_all x2, starting transfers between devices, exchange(): return lax.all_to_all(value, 'row', 0, 0, axis_index_groups=plane)  9.1 us
    ppermute x4, starting transfers between devices, cross(): return lax.ppermute(value, ('row', 'col'), pairs)  8.21 us
  transfers between devices with their start and end apart: 17, of which 9 were waited for; matrix products, arithmetic and copies ran while one was open for 1% of the time, Pallas kernels for 10%

profile of v2, /device:TPU:0, one launch (start us, length us, event | category | flops | bytes accessed | tf_op | source)
XLA Modules:
  0.0 341.9 jit_solution(14367264832239243527)
XLA Ops:
  6.5 1.6 copy.5
  8.1 1.1 fusion
  9.3 0.0 all-gather.7.cloned.1.call-update
  9.3 0.0 all-gather.9.cloned.1.call-start
  9.4 0.7 all-gather.9.cloned.1.call-update
  10.1 0.6 pad_add_fusion.ids
  10.7 56.3 %all-gather.7.cloned.1.call-done.turned = bf16[512,2560]{1,0:T(8,128)(2,1)} async-done(((bf16[128,2560]{1,0:T(8,128)(2,1)}), bf16[512,2560]{1,0:T(8,128)(2,1)}) %all-gather.7.cloned.1.call-update) | async-done | bytes 2621456 | tf_op jit(solution)/shard_map/all_gather | solution.py:285
  67.0 13.3 %send.2 = bf16[512,2560]{1,0:T(8,128)(2,1)} custom-call(s32[3]{0:T(128)} %pad_add_fusion.ids, bf16[512,2560]{1,0:T(8,128)(2,1)} %all-gather.7.cloned.1.call-done.turned, bf16[2560,5120]{1,0:T(8,128)(2,1)} %refs_9_.1), custom_call_target="tpu_custom_call" | custom-call | flops 6710886400 | bytes 15728640 | tf_op jit(solution)/shard_map/send/pallas_call | solution.py:50
  80.3 5.2 %collective-permute-done.refs_0_ = bf16[512,2560]{1,0:T(8,128)(2,1)} collective-permute-done((bf16[512,2560]{1,0:T(8,128)(2,1)}, bf16[512,2560]{1,0:T(8,128)(2,1)}, u32[]{:S(2)}, u32[]{:S(2)}) %collective-permute-start) | collective-permute-done | bytes 2621472 | tf_op jit(solution)/shard_map/ppermute | solution.py:265
  85.5 14.2 %own.2 = (f32[512,640]{1,0:T(8,128)}, bf16[4,512,640]{2,1,0:T(8,128)(2,1)}) custom-call(s32[3]{0:T(128)} %pad_add_fusion.ids, bf16[512,2560]{1,0:T(8,128)(2,1)} %all-gather.7.cloned.1.call-done.turned, bf16[2560,5120]{1,0:T(8,128)(2,1)} %refs_9_.1, bf16[512,2560]{1,0:T(8,128)(2,1)} %collective-permute-done.refs_0_), custom_call_target="tpu_custom_call" | custom-call | flops 6710886400 | bytes 15728640 | tf_op jit(solution)/shard_map/own/pallas_call | solution.py:50
  99.7 4.5 %all-to-all-start = ((bf16[4,512,640]{2,1,0:T(8,128)(2,1)}), bf16[4,512,640]{2,1,0:T(8,128)(2,1)}, u32[]{:S(2)}, u32[]{:S(2)}) async-start(bf16[4,512,640]{2,1,0:T(8,128)(2,1)} %get-tuple-element.13), calls=%async_computation | async-start | bytes 5242880 | tf_op jit(solution)/shard_map/all_to_all | solution.py:280
  104.3 0.0 all-gather.11.cloned.1.call-start
  104.4 17.8 %all-gather.9.cloned.1.call-done.turned = bf16[512,2560]{1,0:T(8,128)(2,1)} async-done(((bf16[128,2560]{1,0:T(8,128)(2,1)}), bf16[512,2560]{1,0:T(8,128)(2,1)}) %all-gather.9.cloned.1.call-update) | async-done | bytes 2621456 | tf_op jit(solution)/shard_map/all_gather | solution.py:285
  122.1 13.2 %send.3 = bf16[512,2560]{1,0:T(8,128)(2,1)} custom-call(s32[3]{0:T(128)} %pad_add_fusion.ids, bf16[512,2560]{1,0:T(8,128)(2,1)} %all-gather.9.cloned.1.call-done.turned, bf16[2560,5120]{1,0:T(8,128)(2,1)} %refs_9_.1), custom_call_target="tpu_custom_call" | custom-call | flops 6710886400 | bytes 15728640 | tf_op jit(solution)/shard_map/send/pallas_call | solution.py:50
  135.3 0.1 all-to-all-done.others
  135.4 3.4 finish.2
  138.8 0.0 all-gather.11.cloned.1.call-update
  138.8 0.0 all-gather.13.cloned.1.call-start
  138.8 1.5 collective-permute-start.3
  140.4 1.4 collective-permute-start.2
  141.8 14.5 %own.3 = (f32[512,640]{1,0:T(8,128)}, bf16[4,512,640]{2,1,0:T(8,128)(2,1)}) custom-call(s32[3]{0:T(128)} %pad_add_fusion.ids, bf16[512,2560]{1,0:T(8,128)(2,1)} %all-gather.9.cloned.1.call-done.turned, bf16[2560,5120]{1,0:T(8,128)(2,1)} %refs_9_.1, bf16[512,2560]{1,0:T(8,128)(2,1)} %collective-permute-done.1.refs_0_), custom_call_target="tpu_custom_call" | custom-call | flops 6710886400 | bytes 15728640 | tf_op jit(solution)/shard_map/own/pallas_call | solution.py:50
  156.2 0.1 collective-permute-done.3
  156.3 1.2 collective-permute-done.2
  157.5 35.3 %all_to_all.15.others = bf16[4,512,640]{2,1,0:T(8,128)(2,1)} all-to-all(bf16[4,512,640]{2,1,0:T(8,128)(2,1)} %get-tuple-element.16), channel_id=1, replica_groups={{0,8,16,24},{4,12,20,28},{1,9,17,25},{5,13,21,29},{2,10,18,26},{6,14,22..., dimensions={0} | all-to-all | bytes 5242880 | tf_op jit(solution)/shard_map/all_to_all | solution.py:280
  192.8 3.3 finish.3
  196.1 0.0 all-gather.13.cloned.1.call-update
  196.1 1.1 slice.19
  197.2 1.0 collective-permute-start.9
  198.2 1.0 slice.18
  199.2 0.6 collective-permute-start.8
  199.8 7.8 %collective-permute-done.9 = bf16[256,640]{1,0:T(8,128)(2,1)S(1)} collective-permute-done((bf16[256,640]{1,0:T(8,128)(2,1)S(1)}, bf16[256,640]{1,0:T(8,128)(2,1)S(1)}, u32[]{:S(2)}, u32[]{:S(2)}) %collective-permute-start.9) | collective-permute-done | bytes 327712 | tf_op jit(solution)/shard_map/ppermute | solution.py:265
  207.7 4.8 %collective-permute-done.8 = bf16[256,640]{1,0:T(8,128)(2,1)S(1)} collective-permute-done((bf16[256,640]{1,0:T(8,128)(2,1)S(1)}, bf16[256,640]{1,0:T(8,128)(2,1)S(1)}, u32[]{:S(2)}, u32[]{:S(2)}) %collective-permute-start.8) | collective-permute-done | bytes 327712 | tf_op jit(solution)/shard_map/ppermute | solution.py:265
  212.5 0.1 maximum_bitcast_fusion
  212.5 1.7 pad_maximum_fusion.refs_10_
  214.2 0.1 collective-permute-start.10
  214.3 0.0 all-gather.11.cloned.1.call-done
  214.3 1.4 copy-done
  215.8 4.5 %all-to-all-start.1 = ((bf16[4,512,640]{2,1,0:T(8,128)(2,1)}), bf16[4,512,640]{2,1,0:T(8,128)(2,1)}, u32[]{:S(2)}, u32[]{:S(2)}) async-start(bf16[4,512,640]{2,1,0:T(8,128)(2,1)} %bitcast.15), calls=%async_computation.1 | async-start | bytes 5242880 | tf_op jit(solution)/shard_map/all_to_all | solution.py:280
  220.3 1.9 collective-permute-start.7
  222.3 1.9 collective-permute-start.6
  224.2 3.5 %collective-permute-start.5 = (bf16[512,640]{1,0:T(8,128)(2,1)S(1)}, bf16[512,640]{1,0:T(8,128)(2,1)S(1)}, u32[]{:S(2)}, u32[]{:S(2)}) collective-permute-start(bf16[512,640]{1,0:T(8,128)(2,1)S(1)} %copy-done.2), channel_id=1, source_target_pairs={{0,1},{1,8},{2,19},{3,26},{4,5},{5,12},{6,23},{7,30},{8,0},{9,9},{... | collective-permute-start | bytes 1966088 | tf_op jit(solution)/shard_map/ppermute | solution.py:274
  227.7 0.9 collective-permute-start.4
  228.6 62.1 %collective-permute-done.7.refs_7_ = bf16[512,640]{1,0:T(8,128)(2,1)S(1)} collective-permute-done((bf16[512,640]{1,0:T(8,128)(2,1)S(1)}, bf16[512,640]{1,0:T(8,128)(2,1)S(1)}, u32[]{:S(2)}, u32[]{:S(2)}) %collective-permute-start.7) | collective-permute-done | bytes 655392 | tf_op jit(solution)/shard_map/ppermute | solution.py:274
  290.7 0.8 copy-done.3
  291.5 0.2 copy-done.4
  291.7 0.2 copy-done.5
  291.9 0.9 copy-done.6
  292.8 42.6 %update.1 = f32[2560,5120]{1,0:T(8,128)} custom-call(s32[3]{0:T(128)} %pad_add_fusion.ids, s32[2]{0:T(128)} %live.1, bf16[4,512,640]{2,1,0:T(8,128)(2,1)} %all-to-all-done.1.refs_0_.refs_1_.refs_2_.refs_3_, bf16[4,512,640]{2,1,0:T(8,128)(2,1)} %all-to-all-done.1.refs_0_.refs_1_.refs_2_.refs_3_, ...), custom_call_target="tpu_custom_call" | custom-call | flops 26843545600 | bytes 89128960 | tf_op jit(solution)/shard_map/update/pallas_call | solution.py:231
  (19 shorter events, 0.0 us)
Async XLA Ops:
  6.5 60.4 %all-gather.7.cloned.1.call-start = ((), (), s32[]{:S(2)}) async-start(), calls=%async_computation.3 | async-start | bytes 3276800 | tf_op jit(solution)/shard_map/all_gather | solution.py:285
  9.3 112.8 %all-gather.9.cloned.1.call-start = ((), (), s32[]{:S(2)}) async-start(), calls=%async_computation.4 | async-start | bytes 3276800 | tf_op jit(solution)/shard_map/all_gather | solution.py:285
  80.3 5.3 %collective-permute-start = (bf16[512,2560]{1,0:T(8,128)(2,1)}, bf16[512,2560]{1,0:T(8,128)(2,1)}, u32[]{:S(2)}, u32[]{:S(2)}) collective-permute-start(bf16[512,2560]{1,0:T(8,128)(2,1)} %send.2), channel_id=1, source_target_pairs={{0,4},{4,0},{8,12},{12,8},{16,20},{20,16},{24,28},{28,24},{1,5},{5... | collective-permute-start | bytes 7864328 | tf_op jit(solution)/shard_map/ppermute | solution.py:265
  99.7 35.7 %all-to-all-start = ((bf16[4,512,640]{2,1,0:T(8,128)(2,1)}), bf16[4,512,640]{2,1,0:T(8,128)(2,1)}, u32[]{:S(2)}, u32[]{:S(2)}) async-start(bf16[4,512,640]{2,1,0:T(8,128)(2,1)} %get-tuple-element.13), calls=%async_computation | async-start | bytes 5242880 | tf_op jit(solution)/shard_map/all_to_all | solution.py:280
  104.3 110.0 %all-gather.11.cloned.1.call-start = ((), (), s32[]{:S(2)}) async-start(), calls=%async_computation.5 | async-start | bytes 3276800 | tf_op jit(solution)/shard_map/all_gather | solution.py:301
  135.3 6.4 %collective-permute-start.1 = (bf16[512,2560]{1,0:T(8,128)(2,1)}, bf16[512,2560]{1,0:T(8,128)(2,1)}, u32[]{:S(2)}, u32[]{:S(2)}) collective-permute-start(bf16[512,2560]{1,0:T(8,128)(2,1)} %send.3), channel_id=1, source_target_pairs={{0,4},{4,0},{8,12},{12,8},{16,20},{20,16},{24,28},{28,24},{1,5},{5... | collective-permute-start | bytes 7864328 | tf_op jit(solution)/shard_map/ppermute | solution.py:265
  138.8 154.0 %all-gather.13.cloned.1.call-start = ((), (), s32[]{:S(2)}) async-start(), calls=%async_computation.6 | async-start | bytes 5898240 | tf_op jit(solution)/shard_map/all_gather | solution.py:290
  138.8 17.5 %collective-permute-start.3 = (bf16[512,640]{1,0:T(8,128)(2,1)}, bf16[512,640]{1,0:T(8,128)(2,1)}, u32[]{:S(2)}, u32[]{:S(2)}) collective-permute-start(bf16[512,640]{1,0:T(8,128)(2,1)} %finish.2), channel_id=1, source_target_pairs={{0,16},{4,20},{8,24},{12,28},{16,0},{20,4},{24,8},{28,12},{1,17},{... | collective-permute-start | bytes 1966088 | tf_op jit(solution)/shard_map/ppermute | solution.py:265
  140.4 17.1 %collective-permute-start.2 = (bf16[512,640]{1,0:T(8,128)(2,1)}, bf16[512,640]{1,0:T(8,128)(2,1)}, u32[]{:S(2)}, u32[]{:S(2)}) collective-permute-start(bf16[512,640]{1,0:T(8,128)(2,1)} %finish.2), channel_id=1, source_target_pairs={{0,8},{4,12},{8,0},{12,4},{16,24},{20,28},{24,16},{28,20},{1,9},{5... | collective-permute-start | bytes 1966088 | tf_op jit(solution)/shard_map/ppermute | solution.py:265
  196.1 16.4 %copy-start.1 = (bf16[512,640]{1,0:T(8,128)(2,1)S(1)}, bf16[512,640]{1,0:T(8,128)(2,1)}, u32[]{:S(2)}) copy-start(bf16[512,640]{1,0:T(8,128)(2,1)} %finish.2) | copy-start | bytes 1966084
  197.2 10.4 %collective-permute-start.9 = (bf16[256,640]{1,0:T(8,128)(2,1)S(1)}, bf16[256,640]{1,0:T(8,128)(2,1)S(1)}, u32[]{:S(2)}, u32[]{:S(2)}) collective-permute-start(bf16[256,640]{1,0:T(8,128)(2,1)S(1)} %slice.19), channel_id=1, source_target_pairs={{0,8},{4,12},{8,0},{12,4},{16,24},{20,28},{24,16},{28,20},{1,9},{5... | collective-permute-start | bytes 983048 | tf_op jit(solution)/shard_map/ppermute | solution.py:265
  199.2 13.3 %collective-permute-start.8 = (bf16[256,640]{1,0:T(8,128)(2,1)S(1)}, bf16[256,640]{1,0:T(8,128)(2,1)S(1)}, u32[]{:S(2)}, u32[]{:S(2)}) collective-permute-start(bf16[256,640]{1,0:T(8,128)(2,1)S(1)} %slice.18), channel_id=1, source_target_pairs={{0,16},{4,20},{8,24},{12,28},{16,0},{20,4},{24,8},{28,12},{1,17},{... | collective-permute-start | bytes 983048 | tf_op jit(solution)/shard_map/ppermute | solution.py:265
  214.2 1.6 copy-start
  214.2 78.6 %collective-permute-start.10 = (bf16[4,512,640]{2,1,0:T(8,128)(2,1)S(1)}, bf16[4,512,640]{2,1,0:T(8,128)(2,1)}, u32[]{:S(2)}, u32[]{:S(2)}) collective-permute-start(bf16[4,512,640]{2,1,0:T(8,128)(2,1)S(1)} %pad_maximum_fusion.refs_10_), channel_id=1, source_target_pairs={{0,4},{4,0},{8,12},{12,8},{16,20},{20,16},{24,28},{28,24},{1,5},{5... | collective-permute-start | bytes 7864328 | tf_op jit(solution)/shard_map/ppermute | solution.py:265
  214.3 6.0 %copy-start.2 = (bf16[512,640]{1,0:T(8,128)(2,1)S(1)}, bf16[512,640]{1,0:T(8,128)(2,1)}, u32[]{:S(2)}) copy-start(bf16[512,640]{1,0:T(8,128)(2,1)} %finish.3) | copy-start | bytes 1966084
  215.8 77.0 %all-to-all-start.1 = ((bf16[4,512,640]{2,1,0:T(8,128)(2,1)}), bf16[4,512,640]{2,1,0:T(8,128)(2,1)}, u32[]{:S(2)}, u32[]{:S(2)}) async-start(bf16[4,512,640]{2,1,0:T(8,128)(2,1)} %bitcast.15), calls=%async_computation.1 | async-start | bytes 5242880 | tf_op jit(solution)/shard_map/all_to_all | solution.py:280
  220.3 70.3 %collective-permute-start.7 = (bf16[512,640]{1,0:T(8,128)(2,1)S(1)}, bf16[512,640]{1,0:T(8,128)(2,1)S(1)}, u32[]{:S(2)}, u32[]{:S(2)}) collective-permute-start(bf16[512,640]{1,0:T(8,128)(2,1)S(1)} %copy-done.2), channel_id=1, source_target_pairs={{0,3},{1,10},{2,17},{3,24},{4,7},{5,14},{6,21},{7,28},{8,2},{9,11}... | collective-permute-start | bytes 1966088 | tf_op jit(solution)/shard_map/ppermute | solution.py:274
  222.3 68.4 %collective-permute-start.6 = (bf16[512,640]{1,0:T(8,128)(2,1)S(1)}, bf16[512,640]{1,0:T(8,128)(2,1)S(1)}, u32[]{:S(2)}, u32[]{:S(2)}) collective-permute-start(bf16[512,640]{1,0:T(8,128)(2,1)S(1)} %copy-done.2), channel_id=1, source_target_pairs={{0,2},{1,11},{2,16},{3,25},{4,6},{5,15},{6,20},{7,29},{8,3},{9,10}... | collective-permute-start | bytes 1966088 | tf_op jit(solution)/shard_map/ppermute | solution.py:274
  224.2 66.5 %collective-permute-start.5 = (bf16[512,640]{1,0:T(8,128)(2,1)S(1)}, bf16[512,640]{1,0:T(8,128)(2,1)S(1)}, u32[]{:S(2)}, u32[]{:S(2)}) collective-permute-start(bf16[512,640]{1,0:T(8,128)(2,1)S(1)} %copy-done.2), channel_id=1, source_target_pairs={{0,1},{1,8},{2,19},{3,26},{4,5},{5,12},{6,23},{7,30},{8,0},{9,9},{... | collective-permute-start | bytes 1966088 | tf_op jit(solution)/shard_map/ppermute | solution.py:274
  227.7 63.0 %collective-permute-start.4 = (bf16[512,640]{1,0:T(8,128)(2,1)S(1)}, bf16[512,640]{1,0:T(8,128)(2,1)S(1)}, u32[]{:S(2)}, u32[]{:S(2)}) collective-permute-start(bf16[512,640]{1,0:T(8,128)(2,1)S(1)} %copy-done.2), channel_id=1, source_target_pairs={{0,0},{1,9},{2,18},{3,27},{4,4},{5,13},{6,22},{7,31},{8,1},{9,8},{... | collective-permute-start | bytes 1966088 | tf_op jit(solution)/shard_map/ppermute | solution.py:274
  290.7 0.8 copy-start.3
  290.7 1.1 copy-start.4
  290.7 1.3 copy-start.5
  291.9 0.9 copy-start.6
Sparse Core Ops, SparseCore 0:
  9.4 57.4 all-gather.6
  68.5 53.5 all-gather.8
  138.9 53.6 all-gather.10
  196.3 74.1 all-gather.12

commit v3 on v2

--- a/solution.py
+++ b/solution.py
@@ -44,27 +44,33 @@
         out[...] = value.astype(BF16)
 
 
+def send_block(cols):
+    return max(b for b in range(128, 513, 128) if cols % b == 0)
+
+
 def stage(kernel, ids, turned, core, mask, others, col_size, twins, out_specs, out_shape):
     slots, rows = turned.shape
-    part = core.shape[1] // twins // col_size
+    cols = core.shape[1] // twins
+    block = cols // col_size if others else send_block(cols)
+    steps = cols // block
     return pl.pallas_call(
         kernel,
         grid_spec=pltpu.PrefetchScalarGridSpec(
             num_scalar_prefetch=1,
-            grid=(col_size,),
+            grid=(steps,),
             in_specs=[
                 pl.BlockSpec((slots, rows), lambda j, ids: (0, 0)),
                 pl.BlockSpec(
-                    (rows, part), lambda j, ids: (0, (ids[1] ^ mask) * col_size + j)
+                    (rows, block), lambda j, ids: (0, (ids[1] ^ mask) * steps + j)
                 ),
             ]
-            + [pl.BlockSpec((slots, part), lambda j, ids: (0, j))] * len(others),
+            + [pl.BlockSpec((slots, block), lambda j, ids: (0, j))] * len(others),
             out_specs=out_specs,
         ),
         out_shape=out_shape,
         cost_estimate=pl.CostEstimate(
-            flops=2 * rows * slots * part * col_size,
-            bytes_accessed=2 * rows * (part * col_size + slots),
+            flops=2 * rows * slots * cols,
+            bytes_accessed=2 * rows * (cols + slots),
             transcendentals=0,
         ),
         compiler_params=pltpu.CompilerParams(vmem_limit_bytes=VMEM),
@@ -92,7 +98,7 @@
                 [],
                 col_size,
                 twins,
-                pl.BlockSpec((slots, part), lambda j, ids: (0, j)),
+                pl.BlockSpec((slots, send_block(part * col_size)), lambda j, ids: (0, j)),
                 jax.ShapeDtypeStruct((slots, part * col_size), BF16),
             )
         result.append((value, flip(value, mask)))

time: 347 us -> 347 us (level)
  transfers between devices with their start and end apart: 17 -> 17, of which waited for: 9 -> 8; matrix products, arithmetic and copies ran while one was open for 1% -> 1% of each run, Pallas kernels for 10% -> 10%
where the time goes in v3:
time: 347 us; the launch traced here: 341 us
  waiting for transfers between devices  156 us (45%)
  Pallas kernels  103 us (30%)
  blocking collectives  35.1 us (10%)
  starting transfers between devices  22.4 us (6%)
  between operations  13.3 us (4%)
  local copies, waits for them, and re-layouts  8.35 us (2%)
    all_gather x2, waiting for transfers between devices, shards(): lax.all_gather(turned[i * half:(i + 1) * half], 'col', axis=0, tiled=True)  74.7 us
    ppermute x4, waiting for transfers between devices, cross(): return lax.ppermute(value, ('row', 'col'), pairs)  62.2 us
    pallas_call x4, Pallas kernels, stage(): pl.pallas_call(kernel, grid_spec=pltpu.PrefetchScalarGridSpec(num_scalar_...  53.9 us
    pallas_call x1, Pallas kernels, update(): pl.pallas_call(functools.partial(update_kernel, masks, twins, spans, plac...  42.6 us
    all_to_all x1, blocking collectives, exchange(): return lax.all_to_all(value, 'row', 0, 0, axis_index_groups=plane)  35.1 us
    ppermute x7, waiting for transfers between devices, flip(): return lax.ppermute(value, 'row', [(r, r ^ mask) for r in range(row_size)])  18.6 us
    all_to_all x2, starting transfers between devices, exchange(): return lax.all_to_all(value, 'row', 0, 0, axis_index_groups=plane)  9.29 us
    ppermute x4, starting transfers between devices, cross(): return lax.ppermute(value, ('row', 'col'), pairs)  8.45 us
  transfers between devices with their start and end apart: 17, of which 8 were waited for; matrix products, arithmetic and copies ran while one was open for 1% of the time, Pallas kernels for 10%

profile of v3, /device:TPU:0, one launch (start us, length us, event | category | flops | bytes accessed | tf_op | source)
XLA Modules:
  0.0 341.2 jit_solution(3576473105131572855)
XLA Ops:
  6.5 1.6 copy.5
  8.1 1.1 fusion
  9.3 0.0 all-gather.7.cloned.1.call-update
  9.3 0.0 all-gather.9.cloned.1.call-start
  9.4 0.7 all-gather.9.cloned.1.call-update
  10.1 0.6 pad_add_fusion.ids
  10.7 56.3 %all-gather.7.cloned.1.call-done.turned = bf16[512,2560]{1,0:T(8,128)(2,1)} async-done(((bf16[128,2560]{1,0:T(8,128)(2,1)}), bf16[512,2560]{1,0:T(8,128)(2,1)}) %all-gather.7.cloned.1.call-update) | async-done | bytes 2621456 | tf_op jit(solution)/shard_map/all_gather | solution.py:291
  67.0 12.7 %send.2 = bf16[512,2560]{1,0:T(8,128)(2,1)} custom-call(s32[3]{0:T(128)} %pad_add_fusion.ids, bf16[512,2560]{1,0:T(8,128)(2,1)} %all-gather.7.cloned.1.call-done.turned, bf16[2560,5120]{1,0:T(8,128)(2,1)} %refs_9_.1), custom_call_target="tpu_custom_call" | custom-call | flops 6710886400 | bytes 15728640 | tf_op jit(solution)/shard_map/send/pallas_call | solution.py:56
  79.7 5.2 %collective-permute-done.refs_0_ = bf16[512,2560]{1,0:T(8,128)(2,1)} collective-permute-done((bf16[512,2560]{1,0:T(8,128)(2,1)}, bf16[512,2560]{1,0:T(8,128)(2,1)}, u32[]{:S(2)}, u32[]{:S(2)}) %collective-permute-start) | collective-permute-done | bytes 2621472 | tf_op jit(solution)/shard_map/ppermute | solution.py:271
  85.0 14.2 %own.2 = (f32[512,640]{1,0:T(8,128)}, bf16[4,512,640]{2,1,0:T(8,128)(2,1)}) custom-call(s32[3]{0:T(128)} %pad_add_fusion.ids, bf16[512,2560]{1,0:T(8,128)(2,1)} %all-gather.7.cloned.1.call-done.turned, bf16[2560,5120]{1,0:T(8,128)(2,1)} %refs_9_.1, bf16[512,2560]{1,0:T(8,128)(2,1)} %collective-permute-done.refs_0_), custom_call_target="tpu_custom_call" | custom-call | flops 6710886400 | bytes 15728640 | tf_op jit(solution)/shard_map/own/pallas_call | solution.py:56
  99.2 4.5 %all-to-all-start = ((bf16[4,512,640]{2,1,0:T(8,128)(2,1)}), bf16[4,512,640]{2,1,0:T(8,128)(2,1)}, u32[]{:S(2)}, u32[]{:S(2)}) async-start(bf16[4,512,640]{2,1,0:T(8,128)(2,1)} %get-tuple-element.13), calls=%async_computation | async-start | bytes 5242880 | tf_op jit(solution)/shard_map/all_to_all | solution.py:286
  103.7 0.0 all-gather.11.cloned.1.call-start
  103.8 18.4 %all-gather.9.cloned.1.call-done.turned = bf16[512,2560]{1,0:T(8,128)(2,1)} async-done(((bf16[128,2560]{1,0:T(8,128)(2,1)}), bf16[512,2560]{1,0:T(8,128)(2,1)}) %all-gather.9.cloned.1.call-update) | async-done | bytes 2621456 | tf_op jit(solution)/shard_map/all_gather | solution.py:291
  122.1 12.5 %send.3 = bf16[512,2560]{1,0:T(8,128)(2,1)} custom-call(s32[3]{0:T(128)} %pad_add_fusion.ids, bf16[512,2560]{1,0:T(8,128)(2,1)} %all-gather.9.cloned.1.call-done.turned, bf16[2560,5120]{1,0:T(8,128)(2,1)} %refs_9_.1), custom_call_target="tpu_custom_call" | custom-call | flops 6710886400 | bytes 15728640 | tf_op jit(solution)/shard_map/send/pallas_call | solution.py:56
  134.7 0.2 all-to-all-done.others
  134.9 3.4 finish.2
  138.2 0.0 all-gather.11.cloned.1.call-update
  138.3 0.0 all-gather.13.cloned.1.call-start
  138.3 1.5 collective-permute-start.3
  139.9 1.3 collective-permute-start.2
  141.1 14.5 %own.3 = (f32[512,640]{1,0:T(8,128)}, bf16[4,512,640]{2,1,0:T(8,128)(2,1)}) custom-call(s32[3]{0:T(128)} %pad_add_fusion.ids, bf16[512,2560]{1,0:T(8,128)(2,1)} %all-gather.9.cloned.1.call-done.turned, bf16[2560,5120]{1,0:T(8,128)(2,1)} %refs_9_.1, bf16[512,2560]{1,0:T(8,128)(2,1)} %collective-permute-done.1.refs_0_), custom_call_target="tpu_custom_call" | custom-call | flops 6710886400 | bytes 15728640 | tf_op jit(solution)/shard_map/own/pallas_call | solution.py:56
  155.6 0.0 collective-permute-done.3
  155.7 1.2 collective-permute-done.2
  156.9 35.1 %all_to_all.15.others = bf16[4,512,640]{2,1,0:T(8,128)(2,1)} all-to-all(bf16[4,512,640]{2,1,0:T(8,128)(2,1)} %get-tuple-element.16), channel_id=1, replica_groups={{0,8,16,24},{4,12,20,28},{1,9,17,25},{5,13,21,29},{2,10,18,26},{6,14,22..., dimensions={0} | all-to-all | bytes 5242880 | tf_op jit(solution)/shard_map/all_to_all | solution.py:286
  192.0 3.3 finish.3
  195.3 0.0 all-gather.13.cloned.1.call-update
  195.4 1.1 slice.19
  196.4 1.0 collective-permute-start.9
  197.4 1.0 slice.18
  198.4 0.7 collective-permute-start.8
  199.1 7.3 %collective-permute-done.9 = bf16[256,640]{1,0:T(8,128)(2,1)S(1)} collective-permute-done((bf16[256,640]{1,0:T(8,128)(2,1)S(1)}, bf16[256,640]{1,0:T(8,128)(2,1)S(1)}, u32[]{:S(2)}, u32[]{:S(2)}) %collective-permute-start.9) | collective-permute-done | bytes 327712 | tf_op jit(solution)/shard_map/ppermute | solution.py:271
  206.4 4.8 %collective-permute-done.8 = bf16[256,640]{1,0:T(8,128)(2,1)S(1)} collective-permute-done((bf16[256,640]{1,0:T(8,128)(2,1)S(1)}, bf16[256,640]{1,0:T(8,128)(2,1)S(1)}, u32[]{:S(2)}, u32[]{:S(2)}) %collective-permute-start.8) | collective-permute-done | bytes 327712 | tf_op jit(solution)/shard_map/ppermute | solution.py:271
  211.2 0.1 maximum_bitcast_fusion
  211.3 1.7 pad_maximum_fusion.refs_10_
  213.0 0.1 collective-permute-start.10
  213.1 0.0 all-gather.11.cloned.1.call-done
  213.1 1.4 copy-done
  214.5 4.7 %all-to-all-start.1 = ((bf16[4,512,640]{2,1,0:T(8,128)(2,1)}), bf16[4,512,640]{2,1,0:T(8,128)(2,1)}, u32[]{:S(2)}, u32[]{:S(2)}) async-start(bf16[4,512,640]{2,1,0:T(8,128)(2,1)} %bitcast.15), calls=%async_computation.1 | async-start | bytes 5242880 | tf_op jit(solution)/shard_map/all_to_all | solution.py:286
  219.3 1.9 collective-permute-start.7
  221.2 1.9 collective-permute-start.6
  223.2 3.7 %collective-permute-start.5 = (bf16[512,640]{1,0:T(8,128)(2,1)S(1)}, bf16[512,640]{1,0:T(8,128)(2,1)S(1)}, u32[]{:S(2)}, u32[]{:S(2)}) collective-permute-start(bf16[512,640]{1,0:T(8,128)(2,1)S(1)} %copy-done.2), channel_id=1, source_target_pairs={{0,1},{1,8},{2,19},{3,26},{4,5},{5,12},{6,23},{7,30},{8,0},{9,9},{... | collective-permute-start | bytes 1966088 | tf_op jit(solution)/shard_map/ppermute | solution.py:280
  226.9 0.9 collective-permute-start.4
  227.8 62.2 %collective-permute-done.7.refs_7_ = bf16[512,640]{1,0:T(8,128)(2,1)S(1)} collective-permute-done((bf16[512,640]{1,0:T(8,128)(2,1)S(1)}, bf16[512,640]{1,0:T(8,128)(2,1)S(1)}, u32[]{:S(2)}, u32[]{:S(2)}) %collective-permute-start.7) | collective-permute-done | bytes 655392 | tf_op jit(solution)/shard_map/ppermute | solution.py:280
  290.0 0.8 copy-done.3
  290.8 0.2 copy-done.4
  291.0 0.2 copy-done.5
  291.2 0.9 copy-done.6
  292.1 42.6 %update.1 = f32[2560,5120]{1,0:T(8,128)} custom-call(s32[3]{0:T(128)} %pad_add_fusion.ids, s32[2]{0:T(128)} %live.1, bf16[4,512,640]{2,1,0:T(8,128)(2,1)} %all-to-all-done.1.refs_0_.refs_1_.refs_2_.refs_3_, bf16[4,512,640]{2,1,0:T(8,128)(2,1)} %all-to-all-done.1.refs_0_.refs_1_.refs_2_.refs_3_, ...), custom_call_target="tpu_custom_call" | custom-call | flops 26843545600 | bytes 89128960 | tf_op jit(solution)/shard_map/update/pallas_call | solution.py:237
  (19 shorter events, 0.0 us)
Async XLA Ops:
  6.5 60.4 %all-gather.7.cloned.1.call-start = ((), (), s32[]{:S(2)}) async-start(), calls=%async_computation.3 | async-start | bytes 3276800 | tf_op jit(solution)/shard_map/all_gather | solution.py:291
  9.3 112.8 %all-gather.9.cloned.1.call-start = ((), (), s32[]{:S(2)}) async-start(), calls=%async_computation.4 | async-start | bytes 3276800 | tf_op jit(solution)/shard_map/all_gather | solution.py:291
  79.7 5.3 %collective-permute-start = (bf16[512,2560]{1,0:T(8,128)(2,1)}, bf16[512,2560]{1,0:T(8,128)(2,1)}, u32[]{:S(2)}, u32[]{:S(2)}) collective-permute-start(bf16[512,2560]{1,0:T(8,128)(2,1)} %send.2), channel_id=1, source_target_pairs={{0,4},{4,0},{8,12},{12,8},{16,20},{20,16},{24,28},{28,24},{1,5},{5... | collective-permute-start | bytes 7864328 | tf_op jit(solution)/shard_map/ppermute | solution.py:271
  99.2 35.7 %all-to-all-start = ((bf16[4,512,640]{2,1,0:T(8,128)(2,1)}), bf16[4,512,640]{2,1,0:T(8,128)(2,1)}, u32[]{:S(2)}, u32[]{:S(2)}) async-start(bf16[4,512,640]{2,1,0:T(8,128)(2,1)} %get-tuple-element.13), calls=%async_computation | async-start | bytes 5242880 | tf_op jit(solution)/shard_map/all_to_all | solution.py:286
  103.7 109.4 %all-gather.11.cloned.1.call-start = ((), (), s32[]{:S(2)}) async-start(), calls=%async_computation.5 | async-start | bytes 3276800 | tf_op jit(solution)/shard_map/all_gather | solution.py:307
  134.7 6.4 %collective-permute-start.1 = (bf16[512,2560]{1,0:T(8,128)(2,1)}, bf16[512,2560]{1,0:T(8,128)(2,1)}, u32[]{:S(2)}, u32[]{:S(2)}) collective-permute-start(bf16[512,2560]{1,0:T(8,128)(2,1)} %send.3), channel_id=1, source_target_pairs={{0,4},{4,0},{8,12},{12,8},{16,20},{20,16},{24,28},{28,24},{1,5},{5... | collective-permute-start | bytes 7864328 | tf_op jit(solution)/shard_map/ppermute | solution.py:271
  138.3 153.8 %all-gather.13.cloned.1.call-start = ((), (), s32[]{:S(2)}) async-start(), calls=%async_computation.6 | async-start | bytes 5898240 | tf_op jit(solution)/shard_map/all_gather | solution.py:296
  138.3 17.3 %collective-permute-start.3 = (bf16[512,640]{1,0:T(8,128)(2,1)}, bf16[512,640]{1,0:T(8,128)(2,1)}, u32[]{:S(2)}, u32[]{:S(2)}) collective-permute-start(bf16[512,640]{1,0:T(8,128)(2,1)} %finish.2), channel_id=1, source_target_pairs={{0,16},{4,20},{8,24},{12,28},{16,0},{20,4},{24,8},{28,12},{1,17},{... | collective-permute-start | bytes 1966088 | tf_op jit(solution)/shard_map/ppermute | solution.py:271
  139.9 17.0 %collective-permute-start.2 = (bf16[512,640]{1,0:T(8,128)(2,1)}, bf16[512,640]{1,0:T(8,128)(2,1)}, u32[]{:S(2)}, u32[]{:S(2)}) collective-permute-start(bf16[512,640]{1,0:T(8,128)(2,1)} %finish.2), channel_id=1, source_target_pairs={{0,8},{4,12},{8,0},{12,4},{16,24},{20,28},{24,16},{28,20},{1,9},{5... | collective-permute-start | bytes 1966088 | tf_op jit(solution)/shard_map/ppermute | solution.py:271
  195.3 15.9 %copy-start.1 = (bf16[512,640]{1,0:T(8,128)(2,1)S(1)}, bf16[512,640]{1,0:T(8,128)(2,1)}, u32[]{:S(2)}) copy-start(bf16[512,640]{1,0:T(8,128)(2,1)} %finish.2) | copy-start | bytes 1966084
  196.4 10.0 %collective-permute-start.9 = (bf16[256,640]{1,0:T(8,128)(2,1)S(1)}, bf16[256,640]{1,0:T(8,128)(2,1)S(1)}, u32[]{:S(2)}, u32[]{:S(2)}) collective-permute-start(bf16[256,640]{1,0:T(8,128)(2,1)S(1)} %slice.19), channel_id=1, source_target_pairs={{0,8},{4,12},{8,0},{12,4},{16,24},{20,28},{24,16},{28,20},{1,9},{5... | collective-permute-start | bytes 983048 | tf_op jit(solution)/shard_map/ppermute | solution.py:271
  198.4 12.8 %collective-permute-start.8 = (bf16[256,640]{1,0:T(8,128)(2,1)S(1)}, bf16[256,640]{1,0:T(8,128)(2,1)S(1)}, u32[]{:S(2)}, u32[]{:S(2)}) collective-permute-start(bf16[256,640]{1,0:T(8,128)(2,1)S(1)} %slice.18), channel_id=1, source_target_pairs={{0,16},{4,20},{8,24},{12,28},{16,0},{20,4},{24,8},{28,12},{1,17},{... | collective-permute-start | bytes 983048 | tf_op jit(solution)/shard_map/ppermute | solution.py:271
  213.0 1.6 copy-start
  213.0 79.1 %collective-permute-start.10 = (bf16[4,512,640]{2,1,0:T(8,128)(2,1)S(1)}, bf16[4,512,640]{2,1,0:T(8,128)(2,1)}, u32[]{:S(2)}, u32[]{:S(2)}) collective-permute-start(bf16[4,512,640]{2,1,0:T(8,128)(2,1)S(1)} %pad_maximum_fusion.refs_10_), channel_id=1, source_target_pairs={{0,4},{4,0},{8,12},{12,8},{16,20},{20,16},{24,28},{28,24},{1,5},{5... | collective-permute-start | bytes 7864328 | tf_op jit(solution)/shard_map/ppermute | solution.py:271
  213.1 6.2 %copy-start.2 = (bf16[512,640]{1,0:T(8,128)(2,1)S(1)}, bf16[512,640]{1,0:T(8,128)(2,1)}, u32[]{:S(2)}) copy-start(bf16[512,640]{1,0:T(8,128)(2,1)} %finish.3) | copy-start | bytes 1966084
  214.5 77.6 %all-to-all-start.1 = ((bf16[4,512,640]{2,1,0:T(8,128)(2,1)}), bf16[4,512,640]{2,1,0:T(8,128)(2,1)}, u32[]{:S(2)}, u32[]{:S(2)}) async-start(bf16[4,512,640]{2,1,0:T(8,128)(2,1)} %bitcast.15), calls=%async_computation.1 | async-start | bytes 5242880 | tf_op jit(solution)/shard_map/all_to_all | solution.py:286
  219.3 70.7 %collective-permute-start.7 = (bf16[512,640]{1,0:T(8,128)(2,1)S(1)}, bf16[512,640]{1,0:T(8,128)(2,1)S(1)}, u32[]{:S(2)}, u32[]{:S(2)}) collective-permute-start(bf16[512,640]{1,0:T(8,128)(2,1)S(1)} %copy-done.2), channel_id=1, source_target_pairs={{0,3},{1,10},{2,17},{3,24},{4,7},{5,14},{6,21},{7,28},{8,2},{9,11}... | collective-permute-start | bytes 1966088 | tf_op jit(solution)/shard_map/ppermute | solution.py:280
  221.2 68.7 %collective-permute-start.6 = (bf16[512,640]{1,0:T(8,128)(2,1)S(1)}, bf16[512,640]{1,0:T(8,128)(2,1)S(1)}, u32[]{:S(2)}, u32[]{:S(2)}) collective-permute-start(bf16[512,640]{1,0:T(8,128)(2,1)S(1)} %copy-done.2), channel_id=1, source_target_pairs={{0,2},{1,11},{2,16},{3,25},{4,6},{5,15},{6,20},{7,29},{8,3},{9,10}... | collective-permute-start | bytes 1966088 | tf_op jit(solution)/shard_map/ppermute | solution.py:280
  223.2 66.8 %collective-permute-start.5 = (bf16[512,640]{1,0:T(8,128)(2,1)S(1)}, bf16[512,640]{1,0:T(8,128)(2,1)S(1)}, u32[]{:S(2)}, u32[]{:S(2)}) collective-permute-start(bf16[512,640]{1,0:T(8,128)(2,1)S(1)} %copy-done.2), channel_id=1, source_target_pairs={{0,1},{1,8},{2,19},{3,26},{4,5},{5,12},{6,23},{7,30},{8,0},{9,9},{... | collective-permute-start | bytes 1966088 | tf_op jit(solution)/shard_map/ppermute | solution.py:280
  226.9 63.1 %collective-permute-start.4 = (bf16[512,640]{1,0:T(8,128)(2,1)S(1)}, bf16[512,640]{1,0:T(8,128)(2,1)S(1)}, u32[]{:S(2)}, u32[]{:S(2)}) collective-permute-start(bf16[512,640]{1,0:T(8,128)(2,1)S(1)} %copy-done.2), channel_id=1, source_target_pairs={{0,0},{1,9},{2,18},{3,27},{4,4},{5,13},{6,22},{7,31},{8,1},{9,8},{... | collective-permute-start | bytes 1966088 | tf_op jit(solution)/shard_map/ppermute | solution.py:280
  290.0 0.8 copy-start.3
  290.0 1.1 copy-start.4
  290.0 1.3 copy-start.5
  291.2 0.9 copy-start.6
Sparse Core Ops, SparseCore 0:
  9.4 57.4 all-gather.6
  68.5 53.5 all-gather.8
  138.4 53.5 all-gather.10
  195.5 88.8 all-gather.12
